TPU v7x, 32 devices: a whole 2x2x4 slice. The times are simulated.
32 devices in a mesh: groups: 2 (over x), tm: 16 (over z, y, core).
Axes of the slice: x: 2, y: 2, z: 4, core: 2. Of those that a mesh axis runs over, the one named last changes fastest.
Arguments:
- state: float32 [32, 64, 1, 1440], P(('groups', 'tm')), parts along dimension 0, may hold values from -18 to 18
- observed: float32 [32, 64, 1, 1440], P(('groups', 'tm')), parts along dimension 0, may hold values from -6 to 6
- obs_mask: int32 [32, 64, 1, 1440], P(('groups', 'tm')), parts along dimension 0, may hold values 0 or 1
- noise: float32 [32, 64, 1, 1440], P(('groups', 'tm')), parts along dimension 0, may hold values from -6 to 6
- w_first: bfloat16 [256, 320, 3, 3], replicated, may hold values from -0.109375 to 0.109375
- b_first: float32 [256], replicated, may hold values from -3 to 3
- w_second: bfloat16 [64, 256, 3, 3], replicated, may hold values from -0.125 to 0.125
- b_second: float32 [64], replicated, may hold values from -3 to 3
Outputs:
- sample: float32 [32, 64, 1, 1440], P(('groups', 'tm')), parts along dimension 0
There are 2 independent parts, one for each index of `groups`. A program takes and returns all parts, laid end to end along the dimension named above; an argument that names none is the same for every part. Nothing has to cross between parts.
All inputs are finite; a program needn't handle non-finite values. No bound on the sum of `obs_mask` on one device may be relied on, other than what follows from the above.
Results may differ from a plain program's by a relative error of at most 0.00048.
Values may be sent and summed in bfloat16 or wider, within the bound.
A program may use at most 64 MiB of HBM per device.

v0:
```python
import jax
import jax.numpy as jnp
from jax import lax
from jax.sharding import PartitionSpec as P


def shifted(value, axis, steps):
    count = lax.axis_size(axis)
    leading, last = (max(0, -steps), min(count, count - steps))
    return lax.ppermute(value, axis, [(source, source + steps) for source in range(leading, last)])


def conv_wrap(field, weights):
    wrapped = jnp.concatenate([field[..., -1:], field, field[..., :1]], axis=-1)
    padded = jnp.pad(wrapped, ((0, 0), (0, 0), (1, 1), (0, 0)))
    return lax.conv_general_dilated(
        padded,
        weights,
        (1, 1),
        "VALID",
        dimension_numbers=("NCHW", "OIHW", "NCHW"),
        preferred_element_type=jnp.float32,
    )


def first_layer(rounded, w_first):
    far_before = shifted(rounded, "tm", 2)
    near_before = shifted(rounded, "tm", 1)
    near_after = shifted(rounded, "tm", -1)
    far_after = shifted(rounded, "tm", -2)
    window = jnp.concatenate([far_before, near_before, rounded, near_after, far_after], axis=1)
    return conv_wrap(window, w_first)


def score(field, observed, mask_f, w_first, b_first, w_second, b_second):
    rounded = field.astype(jnp.bfloat16)
    pre = first_layer(rounded, w_first) + b_first[None, :, None, None]
    hidden = jax.nn.silu(pre).astype(jnp.bfloat16)
    out = conv_wrap(hidden, w_second) + b_second[None, :, None, None]
    return out + mask_f * (observed - field)


def on_device(state, observed, obs_mask, noise, w_first, b_first, w_second, b_second):
    mask_f = obs_mask.astype(jnp.float32)
    predicted = state + 0.5 * score(state, observed, mask_f, w_first, b_first, w_second, b_second)
    drift = score(predicted, observed, mask_f, w_first, b_first, w_second, b_second)
    zsq, gsq = lax.psum((jnp.sum(noise * noise), jnp.sum(drift * drift)), "tm")
    step = 2.0 * 0.16 * 0.16 * zsq / (gsq + 1e-06)
    return predicted + step * drift + jnp.sqrt(2.0 * step) * noise


def solution(mesh):
    return jax.shard_map(
        on_device,
        mesh=mesh,
        in_specs=(
            P(("groups", "tm"), None, None, None),
            P(("groups", "tm"), None, None, None),
            P(("groups", "tm"), None, None, None),
            P(("groups", "tm"), None, None, None),
            P(),
            P(),
            P(),
            P(),
        ),
        out_specs=P(("groups", "tm"), None, None, None),
        check_vma=False,
    )
```

profile of v0, /device:TPU:0, one launch (start us, length us, event | category | flops | bytes accessed | tf_op | source)
XLA Modules:
  0.0 157.0 jit_solution(615614785014657253)
XLA Ops:
  0.0 1.4 convert_element_type.21
  1.4 4.9 %collective-permute-start = (bf16[1,64,1,1440]{3,2,1,0:T(2,128)(2,1)S(1)}, bf16[1,64,1,1440]{3,2,1,0:T(2,128)(2,1)S(1)}, u32[]{:S(2)}, u32[]{:S(2)}) collective-permute-start(bf16[1,64,1,1440]{3,2,1,0:T(2,128)(2,1)S(1)} %convert_element_type.21), channel_id=1, source_target_pairs={{0,2},{1,3},{2,4},{3,5},{4,6},{5,7},{6,8},{7,9},{8,10},{9,11},{10,... | collective-permute-start | bytes 552968 | tf_op jit(solution)/shard_map/ppermute | solution.py:10
  6.3 1.5 collective-permute-start.1
  7.8 1.3 collective-permute-start.2
  9.1 1.3 collective-permute-start.3
  10.4 18.0 %collective-permute-done = bf16[1,64,1,1440]{3,2,1,0:T(2,128)(2,1)S(1)} collective-permute-done((bf16[1,64,1,1440]{3,2,1,0:T(2,128)(2,1)S(1)}, bf16[1,64,1,1440]{3,2,1,0:T(2,128)(2,1)S(1)}, u32[]{:S(2)}, u32[]{:S(2)}) %collective-permute-start) | collective-permute-done | bytes 184352 | tf_op jit(solution)/shard_map/ppermute | solution.py:10
  30.6 1.3 fusion.53
  31.9 13.1 %concatenate.19 = bf16[1,320,1,1442]{3,2,1,0:T(2,128)(2,1)S(1)} concatenate(bf16[1,320,1,1]{3,2,1,0:T(2,128)(2,1)} %get-tuple-element.10, bf16[1,320,1,1440]{3,2,1,0:T(2,128)(2,1)} %copy-done.1, bf16[1,320,1,1]{3,2,1,0:T(2,128)(2,1)} %get-tuple-element.9), dimensions={3} | concatenate | bytes 1845760 | tf_op jit(solution)/shard_map/concatenate | solution.py:14
  45.1 1.0 pad.6
  46.2 3.3 %reshape.50 = bf16[320,1,1,8,181]{4,3,0,2,1:T(8,128)(2,1)S(1)} reshape(bf16[320,1,1,1448]{3,0,2,1:T(8,128)(2,1)} %pad.6) | data formatting | bytes 1853440 | tf_op jit(solution)/shard_map/conv_general_dilated | solution.py:16
  49.5 2.1 %copy.33 = bf16[320,1,1,8,181]{0,3,4,2,1:T(8,128)(2,1)} copy(bf16[320,1,1,8,181]{4,3,0,2,1:T(8,128)(2,1)S(1)} %reshape.50) | data formatting | bytes 1853440 | tf_op jit(solution)/shard_map/conv_general_dilated | solution.py:16
  51.6 0.7 slice.42
  52.3 4.0 %multiply_convert_fusion.1 = bf16[1,8,181,256]{3,1,2,0:T(8,128)(2,1)S(1)} fusion(bf16[256,320,3,3]{0,1,3,2:T(8,128)(2,1)S(1)} %copy-done, bf16[320,1,1,7,2]{0,3,4,2,1:T(8,128)(2,1)S(1)} %slice.42, bf16[320,1,1,8,181]{0,3,4,2,1:T(8,128)(2,1)} %copy.33, f32[256]{0:T(256)S(1)} %copy-done.14, pred[8,181]{0,1:T(8,128)(4,1)S(1)} %copy-done.15), kind=kOutput, calls=%fused_computation.7 | convolution fusion | flops 717126656 | bytes 3154088 | tf_op jit(solution)/shard_map/conv_general_dilated | solution.py:16
  56.5 1.1 reshape.12
  57.6 1.2 slice_bitcast_fusion.1
  58.8 2.8 %concatenate.20 = bf16[1,256,1,1442]{1,3,0,2:T(8,128)(2,1)S(1)} concatenate(bf16[1,256,1,1]{1,3,0,2:T(2,128)(2,1)S(1)} %get-tuple-element.16, bf16[1,256,1,1440]{1,3,0,2:T(8,128)(2,1)S(1)} %slice_bitcast_fusion.1, bf16[1,256,1,1]{1,3,0,2:T(2,128)(2,1)S(1)} %get-tuple-element.15), dimensions={3} | concatenate | bytes 1476608 | tf_op jit(solution)/shard_map/concatenate | solution.py:14
  62.6 1.9 %fusion.18 = f32[1,8,181,64]{3,1,2,0:T(8,128)S(1)} fusion(bf16[64,256,3,3]{1,0,3,2:T(8,128)(2,1)S(1)} %copy-done.13, bf16[256,1,1,7,2]{0,3,4,2,1:T(8,128)(2,1)S(1)} %slice.46, bf16[256,1,1,8,181]{0,3,4,2,1:T(8,128)(2,1)S(1)} %copy.36), kind=kOutput, calls=%fused_computation.21 | convolution fusion | flops 144592896 | bytes 1414144 | tf_op jit(solution)/shard_map/conv_general_dilated | solution.py:16
  65.3 1.0 reshape.31
  66.3 1.9 %fusion.51 = (bf16[1,64,1,1440]{3,1,0,2:T(8,128)(2,1)S(1)}, f32[1,64,1,1440]{3,1,0,2:T(8,128)}) fusion(f32[1,64,1,1440]{3,2,1,0:T(1,128)S(1)} %copy-done.4, s32[1,64,1,1440]{3,2,1,0:T(1,128)S(1)} %copy-done.5, f32[1,1,1448,64]{2,3,1,0:T(8,128)} %reshape.31, f32[1,64,1,1440]{3,2,1,0:T(1,128)S(1)} %copy-done.3), kind=kLoop, calls=%fused_computation.72 | loop fusion | flops 645120 | bytes 2027520 | tf_op jit(solution)/shard_map/convert_element_type | solution.py:36
  68.2 7.2 %collective-permute-start.4 = (bf16[1,64,1,1440]{3,1,0,2:T(8,128)(2,1)S(1)}, bf16[1,64,1,1440]{3,1,0,2:T(8,128)(2,1)S(1)}, u32[]{:S(2)}, u32[]{:S(2)}) collective-permute-start(bf16[1,64,1,1440]{3,1,0,2:T(8,128)(2,1)S(1)} %get-tuple-element.7), channel_id=1, source_target_pairs={{0,2},{1,3},{2,4},{3,5},{4,6},{5,7},{6,8},{7,9},{8,10},{9,11},{10,... | collective-permute-start | bytes 552968 | tf_op jit(solution)/shard_map/ppermute | solution.py:10
  75.5 1.4 multiply_reduce_fusion.1
  76.9 1.3 collective-permute-start.5
  78.2 1.3 collective-permute-start.6
  79.5 1.3 collective-permute-start.7
  80.9 2.0 %collective-permute-done.6 = bf16[1,64,1,1440]{3,1,0,2:T(8,128)(2,1)S(1)} collective-permute-done((bf16[1,64,1,1440]{3,1,0,2:T(8,128)(2,1)S(1)}, bf16[1,64,1,1440]{3,1,0,2:T(8,128)(2,1)S(1)}, u32[]{:S(2)}, u32[]{:S(2)}) %collective-permute-start.6) | collective-permute-done | bytes 184352 | tf_op jit(solution)/shard_map/ppermute | solution.py:10
  82.9 8.5 %collective-permute-done.7 = bf16[1,64,1,1440]{3,1,0,2:T(8,128)(2,1)S(1)} collective-permute-done((bf16[1,64,1,1440]{3,1,0,2:T(8,128)(2,1)S(1)}, bf16[1,64,1,1440]{3,1,0,2:T(8,128)(2,1)S(1)}, u32[]{:S(2)}, u32[]{:S(2)}) %collective-permute-start.7) | collective-permute-done | bytes 184352 | tf_op jit(solution)/shard_map/ppermute | solution.py:10
  91.6 0.9 copy-done.9
  92.4 2.6 %concatenate.22 = bf16[1,320,1,1442]{3,1,0,2:T(8,128)(2,1)S(1)} concatenate(bf16[1,320,1,1]{3,1,0,2:T(8,128)(2,1)S(1)} %get-tuple-element.12, bf16[1,320,1,1440]{3,1,0,2:T(8,128)(2,1)} %copy-done.9, bf16[1,320,1,1]{3,1,0,2:T(8,128)(2,1)S(1)} %get-tuple-element.11), dimensions={3} | concatenate | bytes 1845760 | tf_op jit(solution)/shard_map/concatenate | solution.py:14
  95.1 1.0 pad.10
  96.1 3.3 %reshape.51 = bf16[320,1,1,8,181]{4,3,0,2,1:T(8,128)(2,1)S(1)} reshape(bf16[320,1,1,1448]{3,0,2,1:T(8,128)(2,1)} %pad.10) | data formatting | bytes 1853440 | tf_op jit(solution)/shard_map/conv_general_dilated | solution.py:16
  99.4 2.1 %copy.45 = bf16[320,1,1,8,181]{0,3,4,2,1:T(8,128)(2,1)} copy(bf16[320,1,1,8,181]{4,3,0,2,1:T(8,128)(2,1)S(1)} %reshape.51) | data formatting | bytes 1853440 | tf_op jit(solution)/shard_map/conv_general_dilated | solution.py:16
  101.5 0.7 slice.50
  102.2 4.0 %multiply_convert_fusion = bf16[1,8,181,256]{3,1,2,0:T(8,128)(2,1)S(1)} fusion(bf16[256,320,3,3]{0,1,3,2:T(8,128)(2,1)S(1)} %copy-done, bf16[320,1,1,7,2]{0,3,4,2,1:T(8,128)(2,1)S(1)} %slice.50, bf16[320,1,1,8,181]{0,3,4,2,1:T(8,128)(2,1)} %copy.45, f32[256]{0:T(256)S(1)} %copy-done.14, pred[8,181]{0,1:T(8,128)(4,1)S(1)} %copy-done.15), kind=kOutput, calls=%fused_computation.6 | convolution fusion | flops 717126656 | bytes 3154088 | tf_op jit(solution)/shard_map/conv_general_dilated | solution.py:16
  106.4 1.1 reshape.24
  107.5 1.2 slice_bitcast_fusion
  108.7 0.9 copy-done.8
  109.5 3.8 %concatenate.23 = bf16[1,256,1,1442]{1,3,0,2:T(8,128)(2,1)S(1)} concatenate(bf16[1,256,1,1]{1,3,0,2:T(2,128)(2,1)S(1)} %get-tuple-element.14, bf16[1,256,1,1440]{1,3,0,2:T(8,128)(2,1)} %copy-done.8, bf16[1,256,1,1]{1,3,0,2:T(2,128)(2,1)S(1)} %get-tuple-element.13), dimensions={3} | concatenate | bytes 1476608 | tf_op jit(solution)/shard_map/concatenate | solution.py:14
  113.3 0.9 pad.12
  114.3 1.3 reshape.27
  115.8 1.9 %fusion.22 = f32[1,8,181,64]{3,1,2,0:T(8,128)S(1)} fusion(bf16[64,256,3,3]{1,0,3,2:T(8,128)(2,1)S(1)} %copy-done.13, bf16[256,1,1,7,2]{0,3,4,2,1:T(8,128)(2,1)S(1)} %slice.54, bf16[256,1,1,8,181]{0,3,4,2,1:T(8,128)(2,1)S(1)} %copy.48), kind=kOutput, calls=%fused_computation.24 | convolution fusion | flops 144592896 | bytes 1414144 | tf_op jit(solution)/shard_map/conv_general_dilated | solution.py:16
  117.7 1.2 copy.49
  118.8 1.2 select_add_fusion
  120.1 1.1 copy.50
  121.2 1.3 reshape.33
  122.4 0.7 multiply_reduce_fusion
  123.2 30.1 %all-reduce = (f32[]{:T(128)}, f32[]{:T(128)}) all-reduce(f32[]{:T(128)} %multiply_reduce_fusion.1, f32[]{:T(128)} %multiply_reduce_fusion), channel_id=1, replica_groups=mesh['groups'=2,'tm'=16] {'tm'}, use_global_device_ids=true, to_apply=%region_1.2 | all-reduce | flops 2 | bytes 16 | tf_op jit(solution)/shard_map/psum | solution.py:47
  154.7 1.1 fusion.36
  155.8 1.2 copy.53
  (60 shorter events, 4.6 us)
Async XLA Ops:
  0.0 52.3 %copy-start = (bf16[256,320,3,3]{0,1,3,2:T(8,128)(2,1)S(1)}, bf16[256,320,3,3]{0,1,3,2:T(8,128)(2,1)}, u32[]{:S(2)}) copy-start(bf16[256,320,3,3]{0,1,3,2:T(8,128)(2,1)} %param.12) | copy-start | bytes 4423684
  0.0 29.3 %copy-start.2 = (f32[1,64,1,1440]{3,2,1,0:T(1,128)S(1)}, f32[1,64,1,1440]{3,2,1,0:T(1,128)}, u32[]{:S(2)}) copy-start(f32[1,64,1,1440]{3,2,1,0:T(1,128)} %param.8) | copy-start | bytes 1105924
  1.4 27.0 %collective-permute-start = (bf16[1,64,1,1440]{3,2,1,0:T(2,128)(2,1)S(1)}, bf16[1,64,1,1440]{3,2,1,0:T(2,128)(2,1)S(1)}, u32[]{:S(2)}, u32[]{:S(2)}) collective-permute-start(bf16[1,64,1,1440]{3,2,1,0:T(2,128)(2,1)S(1)} %convert_element_type.21), channel_id=1, source_target_pairs={{0,2},{1,3},{2,4},{3,5},{4,6},{5,7},{6,8},{7,9},{8,10},{9,11},{10,... | collective-permute-start | bytes 552968 | tf_op jit(solution)/shard_map/ppermute | solution.py:10
  6.3 22.5 %collective-permute-start.1 = (bf16[1,64,1,1440]{3,2,1,0:T(2,128)(2,1)S(1)}, bf16[1,64,1,1440]{3,2,1,0:T(2,128)(2,1)S(1)}, u32[]{:S(2)}, u32[]{:S(2)}) collective-permute-start(bf16[1,64,1,1440]{3,2,1,0:T(2,128)(2,1)S(1)} %convert_element_type.21), channel_id=1, source_target_pairs={{0,1},{1,2},{2,3},{3,4},{4,5},{5,6},{6,7},{7,8},{8,9},{9,10},{10,1... | collective-permute-start | bytes 552968 | tf_op jit(solution)/shard_map/ppermute | solution.py:10
  7.8 21.8 %collective-permute-start.2 = (bf16[1,64,1,1440]{3,2,1,0:T(2,128)(2,1)S(1)}, bf16[1,64,1,1440]{3,2,1,0:T(2,128)(2,1)S(1)}, u32[]{:S(2)}, u32[]{:S(2)}) collective-permute-start(bf16[1,64,1,1440]{3,2,1,0:T(2,128)(2,1)S(1)} %convert_element_type.21), channel_id=1, source_target_pairs={{1,0},{2,1},{3,2},{4,3},{5,4},{6,5},{7,6},{8,7},{9,8},{10,9},{11,1... | collective-permute-start | bytes 552968 | tf_op jit(solution)/shard_map/ppermute | solution.py:10
  9.1 21.0 %collective-permute-start.3 = (bf16[1,64,1,1440]{3,2,1,0:T(2,128)(2,1)S(1)}, bf16[1,64,1,1440]{3,2,1,0:T(2,128)(2,1)S(1)}, u32[]{:S(2)}, u32[]{:S(2)}) collective-permute-start(bf16[1,64,1,1440]{3,2,1,0:T(2,128)(2,1)S(1)} %convert_element_type.21), channel_id=1, source_target_pairs={{2,0},{3,1},{4,2},{5,3},{6,4},{7,5},{8,6},{9,7},{10,8},{11,9},{12,... | collective-permute-start | bytes 552968 | tf_op jit(solution)/shard_map/ppermute | solution.py:10
  30.5 1.4 copy-start.1
  49.5 2.9 %copy-start.14 = (f32[256]{0:T(256)S(1)}, f32[256]{0:T(256)}, u32[]{:S(2)}) copy-start(f32[256]{0:T(256)} %param.13) | copy-start | bytes 3076
  49.5 2.8 %copy-start.15 = (pred[8,181]{0,1:T(8,128)(4,1)S(1)}, pred[8,181]{0,1:T(8,128)(4,1)}, u32[]{:S(2)}) copy-start(pred[8,181]{0,1:T(8,128)(4,1)} %constant.40) | copy-start | bytes 4348
  61.6 1.0 copy-start.13
  62.6 2.2 %copy-start.11 = (pred[8,181]{1,0:T(8,128)(4,1)S(1)}, pred[8,181]{1,0:T(8,128)(4,1)}, u32[]{:S(2)}) copy-start(pred[8,181]{1,0:T(8,128)(4,1)} %constant.36) | copy-start | bytes 4348
  62.6 2.3 %copy-start.12 = (f32[64]{0:T(128)S(1)}, f32[64]{0:T(128)}, u32[]{:S(2)}) copy-start(f32[64]{0:T(128)} %param.15) | copy-start | bytes 772
  64.9 1.4 copy-start.3
  64.9 1.4 copy-start.4
  64.9 1.4 copy-start.5
  66.3 9.1 %copy-start.10 = (f32[1,64,1,1440]{3,2,1,0:T(1,128)S(1)}, f32[1,64,1,1440]{3,2,1,0:T(1,128)}, u32[]{:S(2)}) copy-start(f32[1,64,1,1440]{3,2,1,0:T(1,128)} %param.11) | copy-start | bytes 1105924
  68.2 12.5 %collective-permute-start.4 = (bf16[1,64,1,1440]{3,1,0,2:T(8,128)(2,1)S(1)}, bf16[1,64,1,1440]{3,1,0,2:T(8,128)(2,1)S(1)}, u32[]{:S(2)}, u32[]{:S(2)}) collective-permute-start(bf16[1,64,1,1440]{3,1,0,2:T(8,128)(2,1)S(1)} %get-tuple-element.7), channel_id=1, source_target_pairs={{0,2},{1,3},{2,4},{3,5},{4,6},{5,7},{6,8},{7,9},{8,10},{9,11},{10,... | collective-permute-start | bytes 552968 | tf_op jit(solution)/shard_map/ppermute | solution.py:10
  76.9 3.9 %collective-permute-start.5 = (bf16[1,64,1,1440]{3,1,0,2:T(8,128)(2,1)S(1)}, bf16[1,64,1,1440]{3,1,0,2:T(8,128)(2,1)S(1)}, u32[]{:S(2)}, u32[]{:S(2)}) collective-permute-start(bf16[1,64,1,1440]{3,1,0,2:T(8,128)(2,1)S(1)} %get-tuple-element.7), channel_id=1, source_target_pairs={{0,1},{1,2},{2,3},{3,4},{4,5},{5,6},{6,7},{7,8},{8,9},{9,10},{10,1... | collective-permute-start | bytes 552968 | tf_op jit(solution)/shard_map/ppermute | solution.py:10
  78.2 4.7 %collective-permute-start.6 = (bf16[1,64,1,1440]{3,1,0,2:T(8,128)(2,1)S(1)}, bf16[1,64,1,1440]{3,1,0,2:T(8,128)(2,1)S(1)}, u32[]{:S(2)}, u32[]{:S(2)}) collective-permute-start(bf16[1,64,1,1440]{3,1,0,2:T(8,128)(2,1)S(1)} %get-tuple-element.7), channel_id=1, source_target_pairs={{1,0},{2,1},{3,2},{4,3},{5,4},{6,5},{7,6},{8,7},{9,8},{10,9},{11,1... | collective-permute-start | bytes 552968 | tf_op jit(solution)/shard_map/ppermute | solution.py:10
  79.5 12.0 %collective-permute-start.7 = (bf16[1,64,1,1440]{3,1,0,2:T(8,128)(2,1)S(1)}, bf16[1,64,1,1440]{3,1,0,2:T(8,128)(2,1)S(1)}, u32[]{:S(2)}, u32[]{:S(2)}) collective-permute-start(bf16[1,64,1,1440]{3,1,0,2:T(8,128)(2,1)S(1)} %get-tuple-element.7), channel_id=1, source_target_pairs={{2,0},{3,1},{4,2},{5,3},{6,4},{7,5},{8,6},{9,7},{10,8},{11,9},{12,... | collective-permute-start | bytes 552968 | tf_op jit(solution)/shard_map/ppermute | solution.py:10
  91.5 1.0 copy-start.9
  108.6 0.9 copy-start.8
  118.8 3.6 %copy-start.6 = (s32[1,64,1,1440]{3,2,1,0:T(1,128)S(1)}, s32[1,64,1,1440]{3,2,1,0:T(1,128)}, u32[]{:S(2)}) copy-start(s32[1,64,1,1440]{3,2,1,0:T(1,128)} %param.10) | copy-start | bytes 1105924
  118.8 3.6 %copy-start.7 = (f32[1,64,1,1440]{3,1,0,2:T(8,128)S(1)}, f32[1,64,1,1440]{3,1,0,2:T(8,128)}, u32[]{:S(2)}) copy-start(f32[1,64,1,1440]{3,1,0,2:T(8,128)} %get-tuple-element.8) | copy-start | bytes 1105924
where the time goes:
time: 158 us; the launch traced here: 157 us
  local copies, waits for them, and re-layouts  56.3 us (36%)
  blocking collectives  30.1 us (19%)
  waiting for transfers between devices  28.6 us (18%)
  starting transfers between devices  20 us (13%)
  matrix products  11.8 us (7%)
  other arithmetic  8.22 us (5%)
  between operations  1.86 us (1%)
    psum x1, blocking collectives, on_device(): zsq, gsq = lax.psum((jnp.sum(noise * noise), jnp.sum(drift * drift)), 'tm')  30.1 us
    ppermute x8, waiting for transfers between devices, shifted(): lax.ppermute(value, axis, [(source, source + steps) for source in range(l...  28.6 us
    concatenate x8, local copies, waits for them, and re-layouts, conv_wrap(): wrapped = jnp.concatenate([field[..., -1:], field, field[..., :1]], axis=-1)  25.4 us
    ppermute x8, starting transfers between devices, shifted(): lax.ppermute(value, axis, [(source, source + steps) for source in range(l...  20 us
    conv_general_dilated x14, local copies, waits for them, and re-layouts, conv_wrap(): lax.conv_general_dilated(padded, weights, (1, 1), 'VALID', dimension_numb...  15.6 us
    conv_general_dilated x4, matrix products, conv_wrap(): lax.conv_general_dilated(padded, weights, (1, 1), 'VALID', dimension_numb...  11.8 us
    convert_element_type x6, local copies, waits for them, and re-layouts, score(): hidden = jax.nn.silu(pre).astype(jnp.bfloat16)  4.83 us
    unnamed x40, local copies, waits for them, and re-layouts  3.81 us
  transfers between devices with their start and end apart: 8, of which 3 were waited for; matrix products, arithmetic and copies ran while one was open for 2% of the time, Pallas kernels for 0%

commit v1 on v0

v1 whole, which is shorter than its diff:
```python
import functools

import jax
import jax.numpy as jnp
from jax import lax
from jax.experimental import pallas as pl
from jax.experimental.pallas import tpu as pltpu
from jax.sharding import PartitionSpec as P

CHUNKS = 3
LANES = 128


def cut(field, chunks, useful, halo):
    lon = field.shape[-1]
    pieces = []
    for c in range(chunks):
        lo, hi = c * useful - halo, (c + 1) * useful + halo
        parts = []
        if lo < 0:
            parts.append(field[:, lon + lo :])
        parts.append(field[:, max(lo, 0) : min(hi, lon)])
        if hi > lon:
            parts.append(field[:, : hi - lon])
        pieces.append(jnp.concatenate(parts, axis=1) if len(parts) > 1 else parts[0])
    return pieces


def kernel(
    n, chunks, useful, halo,
    state_hbm, obs_hbm, mask_hbm, noise_hbm, w1_hbm, b1_ref, w2_hbm, b2_ref, out_ref,
    state_v, obs_v, mask_v, noise_v, w1_v, w2_v,
    w1t, b1t, b2t, fld, inn, drift, win, sums,
    local_sem, send_sem, recv_sem, sum_send, sum_recv,
):
    me = lax.axis_index("tm")
    group = lax.axis_index("groups")
    core = lax.rem(me, 2)
    par = lax.rem(me // 2, 2)
    sib = me + 1 - 2 * core
    partner = me + 2 - 4 * par
    onward = me + 4 - 8 * par
    near, far = 4 - 4 * par, 4 * par
    relay = 4 - 4 * core
    has_far = jnp.logical_or(jnp.logical_and(par == 0, me >= 4), jnp.logical_and(par == 1, me + 4 < n))
    has_onward = jnp.logical_or(jnp.logical_and(par == 0, me + 4 < n), jnp.logical_and(par == 1, me >= 4))
    nvars = fld.shape[1]
    hid = w1t.shape[0]
    width = fld.shape[2]

    barrier = pltpu.get_barrier_semaphore()

    @pl.loop(1, n)
    def _(d):
        pl.semaphore_signal(
            barrier, inc=1, device_id=(group, lax.rem(me + d, n)), device_id_type=pl.DeviceIdType.MESH
        )

    loads = []
    for i, (src, dst) in enumerate(
        (
            (state_hbm, state_v),
            (w1_hbm.at[w1_hbm.shape[0] // 2], w1_v),
            (w2_hbm.at[w2_hbm.shape[0] // 2], w2_v),
            (obs_hbm, obs_v),
            (mask_hbm, mask_v),
            (noise_hbm, noise_v),
        )
    ):
        loads.append(pltpu.make_async_copy(src, dst, local_sem.at[i]))
        loads[-1].start()

    def remote(step, kind, src, dst, device):
        return pltpu.make_async_remote_copy(
            src_ref=win.at[step, src],
            dst_ref=win.at[step, dst],
            send_sem=send_sem.at[step, kind],
            recv_sem=recv_sem.at[step, kind],
            device_id=(group, device),
            device_id_type=pl.DeviceIdType.MESH,
        )

    def direct(step):
        return remote(step, 0, 2, far, partner)

    def forward(step):
        return remote(step, 1, near, far, onward)

    def own_to_sib(step):
        return remote(step, 2, 2, 1 + 2 * core, sib)

    def relay_to_sib(step):
        return remote(step, 3, relay, 3 - 2 * core, sib)

    @pl.when(jnp.logical_not(has_far))
    def _():
        for step in range(2 * chunks):
            win[step, far] = jnp.zeros((nvars, width), jnp.bfloat16)

    @pl.when(jnp.logical_and(jnp.logical_not(has_far), core == par))
    def _():
        for step in range(2 * chunks):
            win[step, 1 + 2 * core] = jnp.zeros((nvars, width), jnp.bfloat16)

    loads[0].wait()
    for c, piece in enumerate(cut(state_v[...], chunks, useful, halo)):
        fld[c] = piece
        win[c, 2] = piece.astype(jnp.bfloat16)

    pl.semaphore_wait(barrier, n - 1)
    for c in range(chunks):
        direct(c).start()
        own_to_sib(c).start()

    loads[1].wait()
    rows = []
    for slot in range(5):
        for tap in range(3):
            rows.append(w1_v[tap, slot * nvars : (slot + 1) * nvars, :])
    stacked = jnp.concatenate(rows, axis=0).astype(jnp.float32)
    w1t[...] = stacked.T.astype(jnp.bfloat16)
    b1t[...] = jnp.broadcast_to(b1_ref[...], (LANES, hid)).T
    b2t[...] = jnp.broadcast_to(b2_ref[...], (LANES, nvars)).T
    loads[2].wait()
    loads[3].wait()
    loads[4].wait()
    loads[5].wait()
    mask_pieces = cut(mask_v[...].astype(jnp.float32), chunks, useful, halo)
    obs_pieces = cut(obs_v[...], chunks, useful, halo)
    for c in range(chunks):
        inn[0, c] = mask_pieces[c]
        inn[1, c] = obs_pieces[c]
    noise = noise_v[...]
    zsq = jnp.sum(noise * noise)

    def arrive(step):
        direct(step).wait_recv()

        @pl.when(has_onward)
        def _():
            forward(step).start()

        @pl.when(core == par)
        def _():
            relay_to_sib(step).start()

    def arrive_far(step):
        @pl.when(has_far)
        def _():
            forward(step).wait_recv()

            @pl.when(core != par)
            def _():
                relay_to_sib(step).start()

    def work(step):
        own_to_sib(step).wait_recv()

        @pl.when(jnp.logical_or(core != par, has_far))
        def _():
            relay_to_sib(step).wait_recv()

        c = step % chunks
        rows = []
        for slot in range(5):
            x = win[step, slot]
            xf = x.astype(jnp.float32)
            rows.append(pltpu.roll(xf, 1, 1).astype(jnp.bfloat16))
            rows.append(x)
            rows.append(pltpu.roll(xf, width - 1, 1).astype(jnp.bfloat16))
        pre = jnp.dot(w1t[...], jnp.concatenate(rows, axis=0), preferred_element_type=jnp.float32)
        pre = pre + b1t[:, :1]
        hidden = (0.5 * pre * (1.0 + jnp.tanh(0.5 * pre))).astype(jnp.bfloat16)
        y = jnp.dot(
            w2_v[...].reshape(3 * nvars, hid), hidden, preferred_element_type=jnp.float32
        )
        out = pltpu.roll(y[:nvars], 1, 1) + y[nvars : 2 * nvars] + pltpu.roll(y[2 * nvars :], width - 1, 1)
        field = fld[c]
        return field, out + b2t[:, :1] + inn[0, c] * (inn[1, c] - field)

    gsq = jnp.zeros((nvars, width), jnp.float32)
    lane = lax.broadcasted_iota(jnp.int32, (nvars, width), 1)
    valid = jnp.logical_and(lane >= halo, lane < halo + useful)
    steps = 2 * chunks
    for k in range(-2, steps):
        if 0 <= k + 2 < steps:
            arrive(k + 2)
        if 0 <= k + 1 < steps:
            arrive_far(k + 1)
        if k < 0:
            continue
        field, score = work(k)
        if k < chunks:
            field = field + 0.5 * score
            fld[k] = field
            win[k + chunks, 2] = field.astype(jnp.bfloat16)
            direct(k + chunks).start()
            own_to_sib(k + chunks).start()
        else:
            drift[k - chunks] = score
            gsq = gsq + jnp.where(valid, score * score, 0.0)

    row = lax.broadcasted_iota(jnp.int32, (8, LANES), 0)
    sums[me] = jnp.where(row == 0, zsq, jnp.sum(gsq))

    def share(device, slot):
        return pltpu.make_async_remote_copy(
            src_ref=sums.at[me],
            dst_ref=sums.at[slot],
            send_sem=sum_send.at[device],
            recv_sem=sum_recv.at[slot],
            device_id=(group, device),
            device_id_type=pl.DeviceIdType.MESH,
        )

    @pl.loop(1, n)
    def _(d):
        share(lax.rem(me + d, n), me).start()

    @pl.loop(1, n)
    def _(d):
        other = lax.rem(me + d, n)
        share(other, other).wait_recv()

    tot = jnp.sum(sums[...], axis=0)
    zall = tot[0:1, 0:1]
    gall = tot[1:2, 0:1]
    size = 2.0 * 0.16 * 0.16 * zall / (gall + 1e-06)
    scale = jnp.sqrt(2.0 * size)
    for c in range(chunks):
        piece = fld[c] + size * drift[c]
        span = slice(c * useful, (c + 1) * useful)
        out_ref[:, span] = piece[:, halo : halo + useful] + scale * noise_v[:, span]

    @pl.loop(1, n)
    def _(d):
        share(lax.rem(me + d, n), me).wait_send()

    for step in range(steps):
        direct(step).wait_send()
        own_to_sib(step).wait_send()

        @pl.when(has_onward)
        def _():
            forward(step).wait_send()

        @pl.when(jnp.logical_or(core == par, has_far))
        def _():
            relay_to_sib(step).wait_send()


def on_device(n, state, observed, obs_mask, noise, w_first, b_first, w_second, b_second):
    hours, nvars, lat, lon = state.shape
    hid = w_first.shape[0]
    assert hours == 1 and lat == 1 and n % 4 == 0
    assert w_first.shape[1:] == (5 * nvars, 3, 3)
    chunks = CHUNKS
    padded = -(-(lon + 8 * chunks) // (LANES * chunks)) * LANES * chunks
    width = padded // chunks
    assert lon % chunks == 0
    useful = lon // chunks
    halo = (width - useful) // 2
    assert halo >= 4 and useful + 2 * halo == width and halo <= useful
    flat = lambda a: a.reshape(nvars, lon)
    any_spec = pl.BlockSpec(memory_space=pl.ANY)
    vmem = pl.BlockSpec(memory_space=pltpu.VMEM)
    steps = 2 * chunks
    flops = 4 * width * chunks * hid * nvars * (15 + 3)
    out = pl.pallas_call(
        functools.partial(kernel, n, chunks, useful, halo),
        out_shape=jax.ShapeDtypeStruct((nvars, lon), jnp.float32),
        in_specs=[any_spec] * 5 + [vmem, any_spec, vmem],
        out_specs=vmem,
        scratch_shapes=[
            pltpu.VMEM((nvars, lon), jnp.float32),
            pltpu.VMEM((nvars, lon), jnp.float32),
            pltpu.VMEM((nvars, lon), jnp.int32),
            pltpu.VMEM((nvars, lon), jnp.float32),
            pltpu.VMEM((3, 5 * nvars, hid), jnp.bfloat16),
            pltpu.VMEM((3, nvars, hid), jnp.bfloat16),
            pltpu.VMEM((hid, 15 * nvars), jnp.bfloat16),
            pltpu.VMEM((hid, LANES), jnp.float32),
            pltpu.VMEM((nvars, LANES), jnp.float32),
            pltpu.VMEM((chunks, nvars, width), jnp.float32),
            pltpu.VMEM((2, chunks, nvars, width), jnp.float32),
            pltpu.VMEM((chunks, nvars, width), jnp.float32),
            pltpu.VMEM((steps, 5, nvars, width), jnp.bfloat16),
            pltpu.VMEM((n, 8, LANES), jnp.float32),
            pltpu.SemaphoreType.DMA((6,)),
            pltpu.SemaphoreType.DMA((steps, 4)),
            pltpu.SemaphoreType.DMA((steps, 4)),
            pltpu.SemaphoreType.DMA((n,)),
            pltpu.SemaphoreType.DMA((n,)),
        ],
        compiler_params=pltpu.CompilerParams(
            collective_id=0, has_side_effects=True, vmem_limit_bytes=40 * 1024 * 1024
        ),
        cost_estimate=pl.CostEstimate(flops=flops, bytes_accessed=4 * 1024 * 1024, transcendentals=0),
    )(
        flat(state),
        flat(observed),
        flat(obs_mask),
        flat(noise),
        jnp.transpose(w_first, (2, 3, 1, 0)),
        b_first.reshape(1, hid),
        jnp.transpose(w_second, (2, 3, 0, 1)),
        b_second.reshape(1, nvars),
    )
    return out.reshape(state.shape)


def solution(mesh):
    part = P(("groups", "tm"), None, None, None)
    return jax.shard_map(
        functools.partial(on_device, mesh.shape["tm"]),
        mesh=mesh,
        in_specs=(part, part, part, part, P(), P(), P(), P()),
        out_specs=part,
        check_vma=False,
    )
```

time: 158 us -> 40.6 us (0.26)
  local copies, waits for them, and re-layouts: 56.3 us -> 3.42 us
  Pallas kernels: 0 us -> 36.9 us
  blocking collectives: 30.1 us -> 0 us
  waiting for transfers between devices: 28.6 us -> 0 us
  starting transfers between devices: 20 us -> 0 us
  matrix products: 11.8 us -> 0 us
  other arithmetic: 8.22 us -> 0 us
  between operations: 1.86 us -> 0.08 us
    pallas_call x0 -> x1, Pallas kernels: none -> 36.9 us  [on_device(): pl.pallas_call(functools.partial(kernel, n, chunks, useful, halo), out_sh...]
    psum x1 -> x0, blocking collectives: 30.1 us -> none  [on_device(): zsq, gsq = lax.psum((jnp.sum(noise * noise), jnp.sum(drift * drift)), 'tm')]
    ppermute x8 -> x0, waiting for transfers between devices: 28.6 us -> none  [shifted(): lax.ppermute(value, axis, [(source, source + steps) for source in range(l...]
    concatenate x10 -> x0, local copies, waits for them, and re-layouts: 25.9 us -> none  [the longest x8 25.4 us: conv_wrap(): wrapped = jnp.concatenate([field[..., -1:], field, field[..., :1]], axis=-1)]
    ppermute x8 -> x0, starting transfers between devices: 20 us -> none  [shifted(): lax.ppermute(value, axis, [(source, source + steps) for source in range(l...]
    conv_general_dilated x14 -> x0, local copies, waits for them, and re-layouts: 15.6 us -> none  [conv_wrap(): lax.conv_general_dilated(padded, weights, (1, 1), 'VALID', dimension_numb...]
    conv_general_dilated x4 -> x0, matrix products: 11.8 us -> none  [conv_wrap(): lax.conv_general_dilated(padded, weights, (1, 1), 'VALID', dimension_numb...]
    convert_element_type x6 -> x0, local copies, waits for them, and re-layouts: 4.83 us -> none  [score(): hidden = jax.nn.silu(pre).astype(jnp.bfloat16)]
  transfers between devices with their start and end apart: 8 -> 0, of which waited for: 3 -> 0; matrix products, arithmetic and copies ran while one was open for 2% -> 0% of each run, Pallas kernels for 0% -> 0%
where the time goes in v1:
time: 40.6 us; the launch traced here: 40.5 us
  Pallas kernels  36.9 us (91%)
  local copies, waits for them, and re-layouts  3.42 us (8%)
    pallas_call x1, Pallas kernels, on_device(): pl.pallas_call(functools.partial(kernel, n, chunks, useful, halo), out_sh...  36.9 us
    unnamed x15, local copies, waits for them, and re-layouts  2.27 us
    reshape x1, local copies, waits for them, and re-layouts, on_device(): return out.reshape(state.shape)  1.15 us

profile of v1, /device:TPU:0, one launch (start us, length us, event | category | flops | bytes accessed | tf_op | source)
XLA Modules:
  0.0 40.5 jit_solution(7232739220566327371)
XLA Ops:
  0.0 0.0 copy-start.4
  0.0 0.0 copy-start.5
  0.0 0.0 copy-start
  0.0 0.0 copy-start.1
  0.0 0.0 copy-start.2
  0.0 0.0 copy-start.3
  0.0 1.2 %copy.19 = f32[1,64,1,1440]{3,1,2,0:T(8,128)S(1)} copy(f32[1,64,1,1440]{3,2,1,0:T(1,128)} %param.8) | data formatting | bytes 737280
  1.2 1.0 %copy.18 = s32[1,64,1,1440]{3,1,2,0:T(8,128)S(1)} copy(s32[1,64,1,1440]{3,2,1,0:T(1,128)} %param.10) | data formatting | bytes 737280
  2.2 0.0 copy-done.4
  2.2 0.0 copy-done.5
  2.2 0.1 copy_bitcast_fusion
  2.3 0.0 copy-done
  2.3 0.0 copy-done.1
  2.3 0.0 copy-done.2
  2.3 0.0 copy-done.3
  2.3 36.9 %shard_map.82 = f32[64,1440]{1,0:T(8,128)S(1)} custom-call(f32[64,1440]{1,0:T(8,128)S(1)} %bitcast.15, f32[64,1440]{1,0:T(8,128)S(1)} %get-tuple-element.6.obs_hbm, s32[64,1440]{1,0:T(8,128)S(1)} %bitcast.16, f32[64,1440]{1,0:T(8,128)S(1)} %get-tuple-element.5.noise_hbm, bf16[3,3,320,256]{3,2,1,0:T(8,128)(2,1)S(1)} %bitcast.18, f32[1,256]{1,0:T(1,128)S(1)} %bitcast.20, ...), custom_call_target="tpu_custom_call" | custom-call | flops 1811939328 | bytes 4194304 | tf_op jit(solution)/shard_map/pallas_call | solution.py:269
  39.3 1.2 %copy.9 = f32[1,64,1,1440]{3,2,1,0:T(1,128)} copy(f32[1,64,1,1440]{3,1,2,0:T(8,128)S(1)} %bitcast.17) | data formatting | bytes 737280 | tf_op jit(solution)/shard_map/reshape | solution.py:309
Async XLA Ops:
  0.0 2.2 %copy-start.4 = (f32[1,64,1,1440]{3,2,1,0:T(1,128)S(1)}, f32[1,64,1,1440]{3,2,1,0:T(1,128)}, u32[]{:S(2)}) copy-start(f32[1,64,1,1440]{3,2,1,0:T(1,128)} %param.11) | copy-start | bytes 1105924
  0.0 2.2 %copy-start.5 = (f32[1,64,1,1440]{3,2,1,0:T(1,128)S(1)}, f32[1,64,1,1440]{3,2,1,0:T(1,128)}, u32[]{:S(2)}) copy-start(f32[1,64,1,1440]{3,2,1,0:T(1,128)} %param.9) | copy-start | bytes 1105924
  0.0 2.3 %copy-start = (bf16[256,320,3,3]{0,1,3,2:T(8,128)(2,1)S(1)}, bf16[256,320,3,3]{0,1,3,2:T(8,128)(2,1)}, u32[]{:S(2)}) copy-start(bf16[256,320,3,3]{0,1,3,2:T(8,128)(2,1)} %param.12) | copy-start | bytes 4423684
  0.0 2.3 %copy-start.1 = (bf16[64,256,3,3]{1,0,3,2:T(8,128)(2,1)S(1)}, bf16[64,256,3,3]{1,0,3,2:T(8,128)(2,1)}, u32[]{:S(2)}) copy-start(bf16[64,256,3,3]{1,0,3,2:T(8,128)(2,1)} %param.14) | copy-start | bytes 884740
  0.0 2.3 %copy-start.2 = (f32[256]{0:T(256)S(1)}, f32[256]{0:T(256)}, u32[]{:S(2)}) copy-start(f32[256]{0:T(256)} %param.13) | copy-start | bytes 3076
  0.0 2.3 %copy-start.3 = (f32[64]{0:T(128)S(1)}, f32[64]{0:T(128)}, u32[]{:S(2)}) copy-start(f32[64]{0:T(128)} %param.15) | copy-start | bytes 772

commit v2 on v1

--- a/solution.py
+++ b/solution.py
@@ -7,7 +7,7 @@
 from jax.experimental.pallas import tpu as pltpu
 from jax.sharding import PartitionSpec as P
 
-CHUNKS = 3
+CHUNKS = 6
 LANES = 128
 
 

time: 40.6 us -> 39.7 us (0.978)
  Pallas kernels: 36.9 us -> 36.1 us
    pallas_call x1, Pallas kernels: 36.9 us -> 36.1 us  [on_device(): pl.pallas_call(functools.partial(kernel, n, chunks, useful, halo), out_sh...]
where the time goes in v2:
time: 39.7 us; the launch traced here: 39.6 us
  Pallas kernels  36.1 us (91%)
  local copies, waits for them, and re-layouts  3.42 us (9%)
    pallas_call x1, Pallas kernels, on_device(): pl.pallas_call(functools.partial(kernel, n, chunks, useful, halo), out_sh...  36.1 us
    unnamed x15, local copies, waits for them, and re-layouts  2.27 us
    reshape x1, local copies, waits for them, and re-layouts, on_device(): return out.reshape(state.shape)  1.15 us

profile of v2, /device:TPU:0, one launch (start us, length us, event | category | flops | bytes accessed | tf_op | source)
XLA Modules:
  0.0 39.6 jit_solution(8979269635236147181)
XLA Ops:
  0.0 0.0 copy-start.4
  0.0 0.0 copy-start.5
  0.0 0.0 copy-start
  0.0 0.0 copy-start.1
  0.0 0.0 copy-start.2
  0.0 0.0 copy-start.3
  0.0 1.2 %copy.19 = f32[1,64,1,1440]{3,1,2,0:T(8,128)S(1)} copy(f32[1,64,1,1440]{3,2,1,0:T(1,128)} %param.8) | data formatting | bytes 737280
  1.2 1.0 %copy.18 = s32[1,64,1,1440]{3,1,2,0:T(8,128)S(1)} copy(s32[1,64,1,1440]{3,2,1,0:T(1,128)} %param.10) | data formatting | bytes 737280
  2.2 0.0 copy-done.4
  2.2 0.0 copy-done.5
  2.2 0.1 copy_bitcast_fusion
  2.3 0.0 copy-done
  2.3 0.0 copy-done.1
  2.3 0.0 copy-done.2
  2.3 0.0 copy-done.3
  2.3 36.1 %shard_map.82 = f32[64,1440]{1,0:T(8,128)S(1)} custom-call(f32[64,1440]{1,0:T(8,128)S(1)} %bitcast.15, f32[64,1440]{1,0:T(8,128)S(1)} %get-tuple-element.6.obs_hbm, s32[64,1440]{1,0:T(8,128)S(1)} %bitcast.16, f32[64,1440]{1,0:T(8,128)S(1)} %get-tuple-element.5.noise_hbm, bf16[3,3,320,256]{3,2,1,0:T(8,128)(2,1)S(1)} %bitcast.18, f32[1,256]{1,0:T(1,128)S(1)} %bitcast.20, ...), custom_call_target="tpu_custom_call" | custom-call | flops 1811939328 | bytes 4194304 | tf_op jit(solution)/shard_map/pallas_call | solution.py:269
  38.4 1.2 %copy.9 = f32[1,64,1,1440]{3,2,1,0:T(1,128)} copy(f32[1,64,1,1440]{3,1,2,0:T(8,128)S(1)} %bitcast.17) | data formatting | bytes 737280 | tf_op jit(solution)/shard_map/reshape | solution.py:309
Async XLA Ops:
  0.0 2.2 %copy-start.4 = (f32[1,64,1,1440]{3,2,1,0:T(1,128)S(1)}, f32[1,64,1,1440]{3,2,1,0:T(1,128)}, u32[]{:S(2)}) copy-start(f32[1,64,1,1440]{3,2,1,0:T(1,128)} %param.11) | copy-start | bytes 1105924
  0.0 2.2 %copy-start.5 = (f32[1,64,1,1440]{3,2,1,0:T(1,128)S(1)}, f32[1,64,1,1440]{3,2,1,0:T(1,128)}, u32[]{:S(2)}) copy-start(f32[1,64,1,1440]{3,2,1,0:T(1,128)} %param.9) | copy-start | bytes 1105924
  0.0 2.3 %copy-start = (bf16[256,320,3,3]{0,1,3,2:T(8,128)(2,1)S(1)}, bf16[256,320,3,3]{0,1,3,2:T(8,128)(2,1)}, u32[]{:S(2)}) copy-start(bf16[256,320,3,3]{0,1,3,2:T(8,128)(2,1)} %param.12) | copy-start | bytes 4423684
  0.0 2.3 %copy-start.1 = (bf16[64,256,3,3]{1,0,3,2:T(8,128)(2,1)S(1)}, bf16[64,256,3,3]{1,0,3,2:T(8,128)(2,1)}, u32[]{:S(2)}) copy-start(bf16[64,256,3,3]{1,0,3,2:T(8,128)(2,1)} %param.14) | copy-start | bytes 884740
  0.0 2.3 %copy-start.2 = (f32[256]{0:T(256)S(1)}, f32[256]{0:T(256)}, u32[]{:S(2)}) copy-start(f32[256]{0:T(256)} %param.13) | copy-start | bytes 3076
  0.0 2.3 %copy-start.3 = (f32[64]{0:T(128)S(1)}, f32[64]{0:T(128)}, u32[]{:S(2)}) copy-start(f32[64]{0:T(128)} %param.15) | copy-start | bytes 772

commit v3 on v2

--- a/solution.py
+++ b/solution.py
@@ -9,6 +9,7 @@
 
 CHUNKS = 6
 LANES = 128
+ROWS = 16
 
 
 def cut(field, chunks, useful, halo):
@@ -30,7 +31,7 @@
     n, chunks, useful, halo,
     state_hbm, obs_hbm, mask_hbm, noise_hbm, w1_hbm, b1_ref, w2_hbm, b2_ref, out_ref,
     state_v, obs_v, mask_v, noise_v, w1_v, w2_v,
-    w1t, b1t, b2t, fld, inn, drift, win, sums,
+    w1t, b1t, b2t, fld, inn, drift, gacc, win, sums,
     local_sem, send_sem, recv_sem, sum_send, sum_recv,
 ):
     me = lax.axis_index("tm")
@@ -45,8 +46,9 @@
     has_far = jnp.logical_or(jnp.logical_and(par == 0, me >= 4), jnp.logical_and(par == 1, me + 4 < n))
     has_onward = jnp.logical_or(jnp.logical_and(par == 0, me + 4 < n), jnp.logical_and(par == 1, me >= 4))
     nvars = fld.shape[1]
-    hid = w1t.shape[0]
+    hid = w1t.shape[1]
     width = fld.shape[2]
+    steps = 2 * chunks
 
     barrier = pltpu.get_barrier_semaphore()
 
@@ -94,112 +96,125 @@
 
     @pl.when(jnp.logical_not(has_far))
     def _():
-        for step in range(2 * chunks):
+        @pl.loop(0, steps)
+        def _(step):
             win[step, far] = jnp.zeros((nvars, width), jnp.bfloat16)
 
     @pl.when(jnp.logical_and(jnp.logical_not(has_far), core == par))
     def _():
-        for step in range(2 * chunks):
+        @pl.loop(0, steps)
+        def _(step):
             win[step, 1 + 2 * core] = jnp.zeros((nvars, width), jnp.bfloat16)
 
     loads[0].wait()
-    for c, piece in enumerate(cut(state_v[...], chunks, useful, halo)):
-        fld[c] = piece
-        win[c, 2] = piece.astype(jnp.bfloat16)
+
+    @pl.loop(0, nvars // ROWS)
+    def _(i):
+        rows = pl.ds(pl.multiple_of(i * ROWS, ROWS), ROWS)
+        for c, piece in enumerate(cut(state_v[rows, 0, :], chunks, useful, halo)):
+            fld[c, rows] = piece
+            win[c, 2, rows] = piece.astype(jnp.bfloat16)
 
     pl.semaphore_wait(barrier, n - 1)
-    for c in range(chunks):
+
+    @pl.loop(0, chunks)
+    def _(c):
         direct(c).start()
         own_to_sib(c).start()
 
     loads[1].wait()
-    rows = []
-    for slot in range(5):
-        for tap in range(3):
-            rows.append(w1_v[tap, slot * nvars : (slot + 1) * nvars, :])
-    stacked = jnp.concatenate(rows, axis=0).astype(jnp.float32)
-    w1t[...] = stacked.T.astype(jnp.bfloat16)
+
+    @pl.loop(0, 5)
+    def _(slot):
+        rows = pl.ds(pl.multiple_of(slot * nvars, nvars), nvars)
+        stacked = jnp.concatenate([w1_v[tap, rows, :] for tap in range(3)], axis=0)
+        w1t[slot] = stacked.astype(jnp.float32).T.astype(jnp.bfloat16)
+
     b1t[...] = jnp.broadcast_to(b1_ref[...], (LANES, hid)).T
     b2t[...] = jnp.broadcast_to(b2_ref[...], (LANES, nvars)).T
     loads[2].wait()
     loads[3].wait()
     loads[4].wait()
     loads[5].wait()
-    mask_pieces = cut(mask_v[...].astype(jnp.float32), chunks, useful, halo)
-    obs_pieces = cut(obs_v[...], chunks, useful, halo)
-    for c in range(chunks):
-        inn[0, c] = mask_pieces[c]
-        inn[1, c] = obs_pieces[c]
-    noise = noise_v[...]
-    zsq = jnp.sum(noise * noise)
-
-    def arrive(step):
-        direct(step).wait_recv()
-
-        @pl.when(has_onward)
-        def _():
-            forward(step).start()
-
-        @pl.when(core == par)
-        def _():
-            relay_to_sib(step).start()
-
-    def arrive_far(step):
-        @pl.when(has_far)
-        def _():
-            forward(step).wait_recv()
-
-            @pl.when(core != par)
-            def _():
-                relay_to_sib(step).start()
-
-    def work(step):
-        own_to_sib(step).wait_recv()
-
-        @pl.when(jnp.logical_or(core != par, has_far))
-        def _():
-            relay_to_sib(step).wait_recv()
-
-        c = step % chunks
-        rows = []
-        for slot in range(5):
-            x = win[step, slot]
-            xf = x.astype(jnp.float32)
-            rows.append(pltpu.roll(xf, 1, 1).astype(jnp.bfloat16))
-            rows.append(x)
-            rows.append(pltpu.roll(xf, width - 1, 1).astype(jnp.bfloat16))
-        pre = jnp.dot(w1t[...], jnp.concatenate(rows, axis=0), preferred_element_type=jnp.float32)
-        pre = pre + b1t[:, :1]
-        hidden = (0.5 * pre * (1.0 + jnp.tanh(0.5 * pre))).astype(jnp.bfloat16)
-        y = jnp.dot(
-            w2_v[...].reshape(3 * nvars, hid), hidden, preferred_element_type=jnp.float32
-        )
-        out = pltpu.roll(y[:nvars], 1, 1) + y[nvars : 2 * nvars] + pltpu.roll(y[2 * nvars :], width - 1, 1)
-        field = fld[c]
-        return field, out + b2t[:, :1] + inn[0, c] * (inn[1, c] - field)
-
-    gsq = jnp.zeros((nvars, width), jnp.float32)
+
+    def prepare(i, total):
+        rows = pl.ds(pl.multiple_of(i * ROWS, ROWS), ROWS)
+        masks = cut(mask_v[rows, 0, :].astype(jnp.float32), chunks, useful, halo)
+        seen = cut(obs_v[rows, 0, :], chunks, useful, halo)
+        for c in range(chunks):
+            inn[0, c, rows] = masks[c]
+            inn[1, c, rows] = seen[c]
+        noise = noise_v[rows, 0, :]
+        return total + jnp.sum(noise * noise)
+
+    zsq = lax.fori_loop(0, nvars // ROWS, prepare, jnp.float32(0))
+    gacc[...] = jnp.zeros_like(gacc)
+
+    def taps(step, slot):
+        x = win[step, slot]
+        xf = x.astype(jnp.float32)
+        left = pltpu.roll(xf, 1, 1).astype(jnp.bfloat16)
+        right = pltpu.roll(xf, width - 1, 1).astype(jnp.bfloat16)
+        stacked = jnp.concatenate([left, x, right], axis=0)
+        return jnp.dot(w1t[slot], stacked, preferred_element_type=jnp.float32)
+
     lane = lax.broadcasted_iota(jnp.int32, (nvars, width), 1)
     valid = jnp.logical_and(lane >= halo, lane < halo + useful)
-    steps = 2 * chunks
-    for k in range(-2, steps):
-        if 0 <= k + 2 < steps:
-            arrive(k + 2)
-        if 0 <= k + 1 < steps:
-            arrive_far(k + 1)
-        if k < 0:
-            continue
-        field, score = work(k)
-        if k < chunks:
-            field = field + 0.5 * score
-            fld[k] = field
-            win[k + chunks, 2] = field.astype(jnp.bfloat16)
-            direct(k + chunks).start()
-            own_to_sib(k + chunks).start()
-        else:
-            drift[k - chunks] = score
-            gsq = gsq + jnp.where(valid, score * score, 0.0)
-
+
+    @pl.loop(0, steps + 2)
+    def _(turn):
+        @pl.when(turn < steps)
+        def _():
+            direct(turn).wait_recv()
+
+            @pl.when(has_onward)
+            def _():
+                forward(turn).start()
+
+            @pl.when(core == par)
+            def _():
+                relay_to_sib(turn).start()
+
+        @pl.when(jnp.logical_and(has_far, jnp.logical_and(turn >= 1, turn <= steps)))
+        def _():
+            forward(turn - 1).wait_recv()
+
+            @pl.when(core != par)
+            def _():
+                relay_to_sib(turn - 1).start()
+
+        @pl.when(turn >= 2)
+        def _():
+            step = turn - 2
+            c = lax.rem(step, chunks)
+            own_to_sib(step).wait_recv()
+            pre = b1t[:, :1] + taps(step, 2) + taps(step, near) + taps(step, far) + taps(step, 3 - 2 * core)
+
+            @pl.when(jnp.logical_or(core != par, has_far))
+            def _():
+                relay_to_sib(step).wait_recv()
+
+            pre = pre + taps(step, 1 + 2 * core)
+            hidden = (0.5 * pre * (1.0 + jnp.tanh(0.5 * pre))).astype(jnp.bfloat16)
+            y = jnp.dot(w2_v[...].reshape(3 * nvars, hid), hidden, preferred_element_type=jnp.float32)
+            out = pltpu.roll(y[:nvars], 1, 1) + y[nvars : 2 * nvars] + pltpu.roll(y[2 * nvars :], width - 1, 1)
+            field = fld[c]
+            score = out + b2t[:, :1] + inn[0, c] * (inn[1, c] - field)
+
+            @pl.when(step < chunks)
+            def _():
+                moved = field + 0.5 * score
+                fld[c] = moved
+                win[step + chunks, 2] = moved.astype(jnp.bfloat16)
+                direct(step + chunks).start()
+                own_to_sib(step + chunks).start()
+
+            @pl.when(step >= chunks)
+            def _():
+                drift[c] = score
+                gacc[...] += jnp.where(valid, score * score, 0.0)
+
+    gsq = gacc[...]
     row = lax.broadcasted_iota(jnp.int32, (8, LANES), 0)
     sums[me] = jnp.where(row == 0, zsq, jnp.sum(gsq))
 
@@ -227,16 +242,21 @@
     gall = tot[1:2, 0:1]
     size = 2.0 * 0.16 * 0.16 * zall / (gall + 1e-06)
     scale = jnp.sqrt(2.0 * size)
-    for c in range(chunks):
-        piece = fld[c] + size * drift[c]
-        span = slice(c * useful, (c + 1) * useful)
-        out_ref[:, span] = piece[:, halo : halo + useful] + scale * noise_v[:, span]
+
+    @pl.loop(0, nvars // ROWS)
+    def _(i):
+        rows = pl.ds(pl.multiple_of(i * ROWS, ROWS), ROWS)
+        for c in range(chunks):
+            piece = fld[c, rows] + size * drift[c, rows]
+            span = slice(c * useful, (c + 1) * useful)
+            out_ref[rows, span] = piece[:, halo : halo + useful] + scale * noise_v[rows, 0, span]
 
     @pl.loop(1, n)
     def _(d):
         share(lax.rem(me + d, n), me).wait_send()
 
-    for step in range(steps):
+    @pl.loop(0, steps)
+    def _(step):
         direct(step).wait_send()
         own_to_sib(step).wait_send()
 
@@ -261,7 +281,7 @@
     useful = lon // chunks
     halo = (width - useful) // 2
     assert halo >= 4 and useful + 2 * halo == width and halo <= useful
-    flat = lambda a: a.reshape(nvars, lon)
+    flat = lambda a: a.reshape(nvars, 1, lon)
     any_spec = pl.BlockSpec(memory_space=pl.ANY)
     vmem = pl.BlockSpec(memory_space=pltpu.VMEM)
     steps = 2 * chunks
@@ -272,18 +292,19 @@
         in_specs=[any_spec] * 5 + [vmem, any_spec, vmem],
         out_specs=vmem,
         scratch_shapes=[
-            pltpu.VMEM((nvars, lon), jnp.float32),
-            pltpu.VMEM((nvars, lon), jnp.float32),
-            pltpu.VMEM((nvars, lon), jnp.int32),
-            pltpu.VMEM((nvars, lon), jnp.float32),
+            pltpu.VMEM((nvars, 1, lon), jnp.float32),
+            pltpu.VMEM((nvars, 1, lon), jnp.float32),
+            pltpu.VMEM((nvars, 1, lon), jnp.int32),
+            pltpu.VMEM((nvars, 1, lon), jnp.float32),
             pltpu.VMEM((3, 5 * nvars, hid), jnp.bfloat16),
             pltpu.VMEM((3, nvars, hid), jnp.bfloat16),
-            pltpu.VMEM((hid, 15 * nvars), jnp.bfloat16),
+            pltpu.VMEM((5, hid, 3 * nvars), jnp.bfloat16),
             pltpu.VMEM((hid, LANES), jnp.float32),
             pltpu.VMEM((nvars, LANES), jnp.float32),
             pltpu.VMEM((chunks, nvars, width), jnp.float32),
             pltpu.VMEM((2, chunks, nvars, width), jnp.float32),
             pltpu.VMEM((chunks, nvars, width), jnp.float32),
+            pltpu.VMEM((nvars, width), jnp.float32),
             pltpu.VMEM((steps, 5, nvars, width), jnp.bfloat16),
             pltpu.VMEM((n, 8, LANES), jnp.float32),
             pltpu.SemaphoreType.DMA((6,)),
@@ -293,7 +314,7 @@
             pltpu.SemaphoreType.DMA((n,)),
         ],
         compiler_params=pltpu.CompilerParams(
-            collective_id=0, has_side_effects=True, vmem_limit_bytes=40 * 1024 * 1024
+            collective_id=0, has_side_effects=True, vmem_limit_bytes=62 * 1024 * 1024
         ),
         cost_estimate=pl.CostEstimate(flops=flops, bytes_accessed=4 * 1024 * 1024, transcendentals=0),
     )(

time: 39.7 us -> 40.6 us (1.023)
  Pallas kernels: 36.1 us -> 38.2 us
  local copies, waits for them, and re-layouts: 3.42 us -> 2.15 us
    unnamed x15 -> x0, local copies, waits for them, and re-layouts: 2.27 us -> none
    pallas_call x1, Pallas kernels: 36.1 us -> 38.2 us  [on_device(): pl.pallas_call(functools.partial(kernel, n, chunks, useful, halo), out_sh...]
    reshape x1, local copies, waits for them, and re-layouts: 1.15 us -> 2.15 us  [on_device(): return out.reshape(state.shape)]
where the time goes in v3:
time: 40.6 us; the launch traced here: 40.4 us
  Pallas kernels  38.2 us (94%)
  local copies, waits for them, and re-layouts  2.15 us (5%)
    pallas_call x1, Pallas kernels, on_device(): pl.pallas_call(functools.partial(kernel, n, chunks, useful, halo), out_sh...  38.2 us
    reshape x1, local copies, waits for them, and re-layouts, on_device(): return out.reshape(state.shape)  2.15 us

profile of v3, /device:TPU:0, one launch (start us, length us, event | category | flops | bytes accessed | tf_op | source)
XLA Modules:
  0.0 40.4 jit_solution(15966644124706953705)
XLA Ops:
  0.0 38.2 %shard_map.82 = f32[64,1440]{1,0:T(8,128)} custom-call(f32[64,1,1440]{2,1,0:T(1,128)} %bitcast.11, f32[64,1,1440]{2,1,0:T(1,128)} %bitcast.12, s32[64,1,1440]{2,1,0:T(1,128)} %bitcast.13, f32[64,1,1440]{2,1,0:T(1,128)} %bitcast.14, bf16[3,3,320,256]{3,2,1,0:T(8,128)(2,1)} %bitcast.10, f32[1,256]{1,0:T(1,128)} %bitcast.16, bf16[3,3,64,256]{3,2,1,0:T(8,128)(2,1)} %bitcast.15, ...), custom_call_target="tpu_custom_call" | custom-call | flops 1811939328 | bytes 4194304 | tf_op jit(solution)/shard_map/pallas_call | solution.py:289
  38.2 2.1 %copy.9 = f32[1,64,1,1440]{3,2,1,0:T(1,128)} copy(f32[1,64,1,1440]{3,1,2,0:T(8,128)} %bitcast.9) | data formatting | bytes 737280 | tf_op jit(solution)/shard_map/reshape | solution.py:330

commit v4 on v3

--- a/solution.py
+++ b/solution.py
@@ -42,9 +42,10 @@
     partner = me + 2 - 4 * par
     onward = me + 4 - 8 * par
     near, far = 4 - 4 * par, 4 * par
-    relay = 4 - 4 * core
+    cousin = jnp.where(core == par, sib, onward + 1 - 2 * core)
     has_far = jnp.logical_or(jnp.logical_and(par == 0, me >= 4), jnp.logical_and(par == 1, me + 4 < n))
     has_onward = jnp.logical_or(jnp.logical_and(par == 0, me + 4 < n), jnp.logical_and(par == 1, me >= 4))
+    has_cousin = jnp.logical_or(core == par, has_onward)
     nvars = fld.shape[1]
     hid = w1t.shape[1]
     width = fld.shape[2]
@@ -91,8 +92,8 @@
     def own_to_sib(step):
         return remote(step, 2, 2, 1 + 2 * core, sib)
 
-    def relay_to_sib(step):
-        return remote(step, 3, relay, 3 - 2 * core, sib)
+    def relay(step):
+        return remote(step, 3, near, 3 - 2 * core, cousin)
 
     @pl.when(jnp.logical_not(has_far))
     def _():
@@ -161,38 +162,37 @@
     lane = lax.broadcasted_iota(jnp.int32, (nvars, width), 1)
     valid = jnp.logical_and(lane >= halo, lane < halo + useful)
 
-    @pl.loop(0, steps + 2)
+    @pl.loop(0, steps + 1)
     def _(turn):
         @pl.when(turn < steps)
         def _():
             direct(turn).wait_recv()
 
+            @pl.when(has_cousin)
+            def _():
+                relay(turn).start()
+
             @pl.when(has_onward)
             def _():
                 forward(turn).start()
 
-            @pl.when(core == par)
-            def _():
-                relay_to_sib(turn).start()
-
-        @pl.when(jnp.logical_and(has_far, jnp.logical_and(turn >= 1, turn <= steps)))
+        @pl.when(turn >= 1)
         def _():
-            forward(turn - 1).wait_recv()
-
-            @pl.when(core != par)
-            def _():
-                relay_to_sib(turn - 1).start()
-
-        @pl.when(turn >= 2)
-        def _():
-            step = turn - 2
+            step = turn - 1
             c = lax.rem(step, chunks)
+            pre = b1t[:, :1] + taps(step, 2) + taps(step, near)
             own_to_sib(step).wait_recv()
-            pre = b1t[:, :1] + taps(step, 2) + taps(step, near) + taps(step, far) + taps(step, 3 - 2 * core)
+            pre = pre + taps(step, 3 - 2 * core)
+
+            @pl.when(has_far)
+            def _():
+                forward(step).wait_recv()
+
+            pre = pre + taps(step, far)
 
             @pl.when(jnp.logical_or(core != par, has_far))
             def _():
-                relay_to_sib(step).wait_recv()
+                relay(step).wait_recv()
 
             pre = pre + taps(step, 1 + 2 * core)
             hidden = (0.5 * pre * (1.0 + jnp.tanh(0.5 * pre))).astype(jnp.bfloat16)
@@ -249,7 +249,7 @@
         for c in range(chunks):
             piece = fld[c, rows] + size * drift[c, rows]
             span = slice(c * useful, (c + 1) * useful)
-            out_ref[rows, span] = piece[:, halo : halo + useful] + scale * noise_v[rows, 0, span]
+            out_ref[rows, 0, span] = piece[:, halo : halo + useful] + scale * noise_v[rows, 0, span]
 
     @pl.loop(1, n)
     def _(d):
@@ -264,9 +264,9 @@
         def _():
             forward(step).wait_send()
 
-        @pl.when(jnp.logical_or(core == par, has_far))
+        @pl.when(has_cousin)
         def _():
-            relay_to_sib(step).wait_send()
+            relay(step).wait_send()
 
 
 def on_device(n, state, observed, obs_mask, noise, w_first, b_first, w_second, b_second):
@@ -288,7 +288,7 @@
     flops = 4 * width * chunks * hid * nvars * (15 + 3)
     out = pl.pallas_call(
         functools.partial(kernel, n, chunks, useful, halo),
-        out_shape=jax.ShapeDtypeStruct((nvars, lon), jnp.float32),
+        out_shape=jax.ShapeDtypeStruct((nvars, 1, lon), jnp.float32),
         in_specs=[any_spec] * 5 + [vmem, any_spec, vmem],
         out_specs=vmem,
         scratch_shapes=[

time: 40.6 us -> 39.1 us (0.963)
  Pallas kernels: 38.2 us -> 37.1 us
    reshape x1 -> x0, local copies, waits for them, and re-layouts: 2.15 us -> none  [on_device(): return out.reshape(state.shape)]
    unnamed x0 -> x1, local copies, waits for them, and re-layouts: none -> 1.78 us
    pallas_call x1, Pallas kernels: 38.2 us -> 37.1 us  [on_device(): pl.pallas_call(functools.partial(kernel, n, chunks, useful, halo), out_sh...]
where the time goes in v4:
time: 39.1 us; the launch traced here: 38.9 us
  Pallas kernels  37.1 us (95%)
  local copies, waits for them, and re-layouts  1.78 us (5%)
    pallas_call x1, Pallas kernels, on_device(): pl.pallas_call(functools.partial(kernel, n, chunks, useful, halo), out_sh...  37.1 us
    unnamed x1, local copies, waits for them, and re-layouts  1.78 us

profile of v4, /device:TPU:0, one launch (start us, length us, event | category | flops | bytes accessed | tf_op | source)
XLA Modules:
  0.0 38.9 jit_solution(13400626286253911242)
XLA Ops:
  0.0 37.1 %shard_map.82 = f32[64,1,1440]{2,1,0:T(1,128)} custom-call(f32[64,1,1440]{2,1,0:T(1,128)} %bitcast.11, f32[64,1,1440]{2,1,0:T(1,128)} %bitcast.12, s32[64,1,1440]{2,1,0:T(1,128)} %bitcast.13, f32[64,1,1440]{2,1,0:T(1,128)} %bitcast.14, bf16[3,3,320,256]{3,2,1,0:T(8,128)(2,1)} %bitcast.10, f32[1,256]{1,0:T(1,128)} %bitcast.16, ...), custom_call_target="tpu_custom_call" | custom-call | flops 1811939328 | bytes 4194304 | tf_op jit(solution)/shard_map/pallas_call | solution.py:289
  37.1 1.8 %copy.10 = f32[1,64,1,1440]{3,2,1,0:T(1,128)} copy(f32[1,64,1,1440]{3,2,1,0:T(1,128)} %bitcast.9) | data formatting | bytes 737280

commit v5 on v4

--- a/solution.py
+++ b/solution.py
@@ -7,7 +7,7 @@
 from jax.experimental.pallas import tpu as pltpu
 from jax.sharding import PartitionSpec as P
 
-CHUNKS = 6
+CHUNKS = 3
 LANES = 128
 ROWS = 16
 
@@ -47,7 +47,7 @@
     has_onward = jnp.logical_or(jnp.logical_and(par == 0, me + 4 < n), jnp.logical_and(par == 1, me >= 4))
     has_cousin = jnp.logical_or(core == par, has_onward)
     nvars = fld.shape[1]
-    hid = w1t.shape[1]
+    hid = w1t.shape[0]
     width = fld.shape[2]
     steps = 2 * chunks
 
@@ -125,11 +125,10 @@
 
     loads[1].wait()
 
-    @pl.loop(0, 5)
-    def _(slot):
-        rows = pl.ds(pl.multiple_of(slot * nvars, nvars), nvars)
+    for slot in range(5):
+        rows = slice(slot * nvars, (slot + 1) * nvars)
         stacked = jnp.concatenate([w1_v[tap, rows, :] for tap in range(3)], axis=0)
-        w1t[slot] = stacked.astype(jnp.float32).T.astype(jnp.bfloat16)
+        w1t[:, slot * 3 * nvars : (slot + 1) * 3 * nvars] = stacked.astype(jnp.float32).T.astype(jnp.bfloat16)
 
     b1t[...] = jnp.broadcast_to(b1_ref[...], (LANES, hid)).T
     b2t[...] = jnp.broadcast_to(b2_ref[...], (LANES, nvars)).T
@@ -154,10 +153,7 @@
     def taps(step, slot):
         x = win[step, slot]
         xf = x.astype(jnp.float32)
-        left = pltpu.roll(xf, 1, 1).astype(jnp.bfloat16)
-        right = pltpu.roll(xf, width - 1, 1).astype(jnp.bfloat16)
-        stacked = jnp.concatenate([left, x, right], axis=0)
-        return jnp.dot(w1t[slot], stacked, preferred_element_type=jnp.float32)
+        return [pltpu.roll(xf, 1, 1).astype(jnp.bfloat16), x, pltpu.roll(xf, width - 1, 1).astype(jnp.bfloat16)]
 
     lane = lax.broadcasted_iota(jnp.int32, (nvars, width), 1)
     valid = jnp.logical_and(lane >= halo, lane < halo + useful)
@@ -180,21 +176,18 @@
         def _():
             step = turn - 1
             c = lax.rem(step, chunks)
-            pre = b1t[:, :1] + taps(step, 2) + taps(step, near)
             own_to_sib(step).wait_recv()
-            pre = pre + taps(step, 3 - 2 * core)
 
             @pl.when(has_far)
             def _():
                 forward(step).wait_recv()
 
-            pre = pre + taps(step, far)
-
             @pl.when(jnp.logical_or(core != par, has_far))
             def _():
                 relay(step).wait_recv()
 
-            pre = pre + taps(step, 1 + 2 * core)
+            stacked = jnp.concatenate([row for slot in range(5) for row in taps(step, slot)], axis=0)
+            pre = jnp.dot(w1t[...], stacked, preferred_element_type=jnp.float32) + b1t[:, :1]
             hidden = (0.5 * pre * (1.0 + jnp.tanh(0.5 * pre))).astype(jnp.bfloat16)
             y = jnp.dot(w2_v[...].reshape(3 * nvars, hid), hidden, preferred_element_type=jnp.float32)
             out = pltpu.roll(y[:nvars], 1, 1) + y[nvars : 2 * nvars] + pltpu.roll(y[2 * nvars :], width - 1, 1)
@@ -298,7 +291,7 @@
             pltpu.VMEM((nvars, 1, lon), jnp.float32),
             pltpu.VMEM((3, 5 * nvars, hid), jnp.bfloat16),
             pltpu.VMEM((3, nvars, hid), jnp.bfloat16),
-            pltpu.VMEM((5, hid, 3 * nvars), jnp.bfloat16),
+            pltpu.VMEM((hid, 15 * nvars), jnp.bfloat16),
             pltpu.VMEM((hid, LANES), jnp.float32),
             pltpu.VMEM((nvars, LANES), jnp.float32),
             pltpu.VMEM((chunks, nvars, width), jnp.float32),

time: 39.1 us -> 37 us (0.946)
  Pallas kernels: 37.1 us -> 35 us
    pallas_call x1, Pallas kernels: 37.1 us -> 35 us  [on_device(): pl.pallas_call(functools.partial(kernel, n, chunks, useful, halo), out_sh...]
where the time goes in v5:
time: 37 us; the launch traced here: 36.8 us
  Pallas kernels  35 us (95%)
  local copies, waits for them, and re-layouts  1.78 us (5%)
    pallas_call x1, Pallas kernels, on_device(): pl.pallas_call(functools.partial(kernel, n, chunks, useful, halo), out_sh...  35 us
    unnamed x1, local copies, waits for them, and re-layouts  1.78 us

profile of v5, /device:TPU:0, one launch (start us, length us, event | category | flops | bytes accessed | tf_op | source)
XLA Modules:
  0.0 36.8 jit_solution(18040190835240531639)
XLA Ops:
  0.0 35.0 %shard_map.82 = f32[64,1,1440]{2,1,0:T(1,128)} custom-call(f32[64,1,1440]{2,1,0:T(1,128)} %bitcast.11, f32[64,1,1440]{2,1,0:T(1,128)} %bitcast.12, s32[64,1,1440]{2,1,0:T(1,128)} %bitcast.13, f32[64,1,1440]{2,1,0:T(1,128)} %bitcast.14, bf16[3,3,320,256]{3,2,1,0:T(8,128)(2,1)} %bitcast.10, f32[1,256]{1,0:T(1,128)} %bitcast.16, ...), custom_call_target="tpu_custom_call" | custom-call | flops 1811939328 | bytes 4194304 | tf_op jit(solution)/shard_map/pallas_call | solution.py:282
  35.0 1.8 %copy.10 = f32[1,64,1,1440]{3,2,1,0:T(1,128)} copy(f32[1,64,1,1440]{3,2,1,0:T(1,128)} %bitcast.9) | data formatting | bytes 737280

commit v6 on v5

--- a/solution.py
+++ b/solution.py
@@ -31,7 +31,7 @@
     n, chunks, useful, halo,
     state_hbm, obs_hbm, mask_hbm, noise_hbm, w1_hbm, b1_ref, w2_hbm, b2_ref, out_ref,
     state_v, obs_v, mask_v, noise_v, w1_v, w2_v,
-    w1t, b1t, b2t, fld, inn, drift, gacc, win, sums,
+    w1t, b1t, b2t, fld, inn, drift, gacc, acc, whole, win, sums,
     local_sem, send_sem, recv_sem, sum_send, sum_recv,
 ):
     me = lax.axis_index("tm")
@@ -53,12 +53,6 @@
 
     barrier = pltpu.get_barrier_semaphore()
 
-    @pl.loop(1, n)
-    def _(d):
-        pl.semaphore_signal(
-            barrier, inc=1, device_id=(group, lax.rem(me + d, n)), device_id_type=pl.DeviceIdType.MESH
-        )
-
     loads = []
     for i, (src, dst) in enumerate(
         (
@@ -73,6 +67,12 @@
         loads.append(pltpu.make_async_copy(src, dst, local_sem.at[i]))
         loads[-1].start()
 
+    @pl.loop(1, n)
+    def _(d):
+        pl.semaphore_signal(
+            barrier, inc=1, device_id=(group, lax.rem(me + d, n)), device_id_type=pl.DeviceIdType.MESH
+        )
+
     def remote(step, kind, src, dst, device):
         return pltpu.make_async_remote_copy(
             src_ref=win.at[step, src],
@@ -125,10 +125,11 @@
 
     loads[1].wait()
 
-    for slot in range(5):
-        rows = slice(slot * nvars, (slot + 1) * nvars)
+    roles = (2, 3 - 2 * core, near, far, 1 + 2 * core)
+    for role, slot in enumerate(roles):
+        rows = pl.ds(pl.multiple_of(slot * nvars, nvars), nvars)
         stacked = jnp.concatenate([w1_v[tap, rows, :] for tap in range(3)], axis=0)
-        w1t[:, slot * 3 * nvars : (slot + 1) * 3 * nvars] = stacked.astype(jnp.float32).T.astype(jnp.bfloat16)
+        w1t[:, role * 3 * nvars : (role + 1) * 3 * nvars] = stacked.astype(jnp.float32).T.astype(jnp.bfloat16)
 
     b1t[...] = jnp.broadcast_to(b1_ref[...], (LANES, hid)).T
     b2t[...] = jnp.broadcast_to(b2_ref[...], (LANES, nvars)).T
@@ -145,6 +146,7 @@
             inn[0, c, rows] = masks[c]
             inn[1, c, rows] = seen[c]
         noise = noise_v[rows, 0, :]
+        whole[2, rows] = noise
         return total + jnp.sum(noise * noise)
 
     zsq = lax.fori_loop(0, nvars // ROWS, prepare, jnp.float32(0))
@@ -154,6 +156,20 @@
         x = win[step, slot]
         xf = x.astype(jnp.float32)
         return [pltpu.roll(xf, 1, 1).astype(jnp.bfloat16), x, pltpu.roll(xf, width - 1, 1).astype(jnp.bfloat16)]
+
+    split = 2 * 3 * nvars
+
+    def product(step, first, last, weights):
+        stacked = jnp.concatenate([row for role in range(first, last) for row in taps(step, roles[role])], axis=0)
+        return jnp.dot(weights, stacked, preferred_element_type=jnp.float32)
+
+    def begin(step, c):
+        own_to_sib(step).wait_recv()
+        acc[c] = product(step, 0, 2, w1t[:, :split]) + b1t[:, :1]
+
+    @pl.loop(0, chunks)
+    def _(c):
+        begin(c, c)
 
     lane = lax.broadcasted_iota(jnp.int32, (nvars, width), 1)
     valid = jnp.logical_and(lane >= halo, lane < halo + useful)
@@ -176,7 +192,10 @@
         def _():
             step = turn - 1
             c = lax.rem(step, chunks)
-            own_to_sib(step).wait_recv()
+
+            @pl.when(step >= chunks)
+            def _():
+                begin(step, c)
 
             @pl.when(has_far)
             def _():
@@ -186,8 +205,7 @@
             def _():
                 relay(step).wait_recv()
 
-            stacked = jnp.concatenate([row for slot in range(5) for row in taps(step, slot)], axis=0)
-            pre = jnp.dot(w1t[...], stacked, preferred_element_type=jnp.float32) + b1t[:, :1]
+            pre = acc[c] + product(step, 2, 5, w1t[:, split:])
             hidden = (0.5 * pre * (1.0 + jnp.tanh(0.5 * pre))).astype(jnp.bfloat16)
             y = jnp.dot(w2_v[...].reshape(3 * nvars, hid), hidden, preferred_element_type=jnp.float32)
             out = pltpu.roll(y[:nvars], 1, 1) + y[nvars : 2 * nvars] + pltpu.roll(y[2 * nvars :], width - 1, 1)
@@ -225,6 +243,14 @@
     def _(d):
         share(lax.rem(me + d, n), me).start()
 
+    @pl.loop(0, nvars // ROWS)
+    def _(i):
+        rows = pl.ds(pl.multiple_of(i * ROWS, ROWS), ROWS)
+        for c in range(chunks):
+            span = slice(c * useful, (c + 1) * useful)
+            whole[0, rows, span] = fld[c, rows, halo : halo + useful]
+            whole[1, rows, span] = drift[c, rows, halo : halo + useful]
+
     @pl.loop(1, n)
     def _(d):
         other = lax.rem(me + d, n)
@@ -239,10 +265,7 @@
     @pl.loop(0, nvars // ROWS)
     def _(i):
         rows = pl.ds(pl.multiple_of(i * ROWS, ROWS), ROWS)
-        for c in range(chunks):
-            piece = fld[c, rows] + size * drift[c, rows]
-            span = slice(c * useful, (c + 1) * useful)
-            out_ref[rows, 0, span] = piece[:, halo : halo + useful] + scale * noise_v[rows, 0, span]
+        out_ref[rows, 0, :] = whole[0, rows] + size * whole[1, rows] + scale * whole[2, rows]
 
     @pl.loop(1, n)
     def _(d):
@@ -298,6 +321,8 @@
             pltpu.VMEM((2, chunks, nvars, width), jnp.float32),
             pltpu.VMEM((chunks, nvars, width), jnp.float32),
             pltpu.VMEM((nvars, width), jnp.float32),
+            pltpu.VMEM((chunks, hid, width), jnp.float32),
+            pltpu.VMEM((3, nvars, lon), jnp.float32),
             pltpu.VMEM((steps, 5, nvars, width), jnp.bfloat16),
             pltpu.VMEM((n, 8, LANES), jnp.float32),
             pltpu.SemaphoreType.DMA((6,)),

time: 37 us -> 36.5 us (0.986)
  Pallas kernels: 35 us -> 34.5 us
    pallas_call x1, Pallas kernels: 35 us -> 34.5 us  [on_device(): pl.pallas_call(functools.partial(kernel, n, chunks, useful, halo), out_sh...]
where the time goes in v6:
time: 36.5 us; the launch traced here: 36.3 us
  Pallas kernels  34.5 us (95%)
  local copies, waits for them, and re-layouts  1.78 us (5%)
    pallas_call x1, Pallas kernels, on_device(): pl.pallas_call(functools.partial(kernel, n, chunks, useful, halo), out_sh...  34.5 us
    unnamed x1, local copies, waits for them, and re-layouts  1.78 us

profile of v6, /device:TPU:0, one launch (start us, length us, event | category | flops | bytes accessed | tf_op | source)
XLA Modules:
  0.0 36.3 jit_solution(1994298487414682385)
XLA Ops:
  0.0 34.5 %shard_map.82 = f32[64,1,1440]{2,1,0:T(1,128)} custom-call(f32[64,1,1440]{2,1,0:T(1,128)} %bitcast.11, f32[64,1,1440]{2,1,0:T(1,128)} %bitcast.12, s32[64,1,1440]{2,1,0:T(1,128)} %bitcast.13, f32[64,1,1440]{2,1,0:T(1,128)} %bitcast.14, bf16[3,3,320,256]{3,2,1,0:T(8,128)(2,1)} %bitcast.10, f32[1,256]{1,0:T(1,128)} %bitcast.16, ...), custom_call_target="tpu_custom_call" | custom-call | flops 1811939328 | bytes 4194304 | tf_op jit(solution)/shard_map/pallas_call | solution.py:305
  34.5 1.8 %copy.10 = f32[1,64,1,1440]{3,2,1,0:T(1,128)} copy(f32[1,64,1,1440]{3,2,1,0:T(1,128)} %bitcast.9) | data formatting | bytes 737280

commit v7 on v6

--- a/solution.py
+++ b/solution.py
@@ -1,4 +1,5 @@
 import functools
+import math
 
 import jax
 import jax.numpy as jnp
@@ -10,6 +11,7 @@
 CHUNKS = 3
 LANES = 128
 ROWS = 16
+RADIX = 4
 
 
 def cut(field, chunks, useful, halo):
@@ -41,6 +43,7 @@
     sib = me + 1 - 2 * core
     partner = me + 2 - 4 * par
     onward = me + 4 - 8 * par
+    source = me - 4 + 8 * par
     near, far = 4 - 4 * par, 4 * par
     cousin = jnp.where(core == par, sib, onward + 1 - 2 * core)
     has_far = jnp.logical_or(jnp.logical_and(par == 0, me >= 4), jnp.logical_and(par == 1, me + 4 < n))
@@ -67,11 +70,26 @@
         loads.append(pltpu.make_async_copy(src, dst, local_sem.at[i]))
         loads[-1].start()
 
-    @pl.loop(1, n)
-    def _(d):
-        pl.semaphore_signal(
-            barrier, inc=1, device_id=(group, lax.rem(me + d, n)), device_id_type=pl.DeviceIdType.MESH
-        )
+    strides = [RADIX**i for i in range(round(math.log(n, RADIX)))]
+
+    def peer(stride, turn):
+        digit = lax.rem(me // stride, RADIX)
+        return me + (lax.rem(digit + turn, RADIX) - digit) * stride
+
+    def greet(device):
+        pl.semaphore_signal(barrier, inc=1, device_id=(group, device), device_id_type=pl.DeviceIdType.MESH)
+
+    for stride in strides:
+        for turn in range(1, RADIX):
+            greet(peer(stride, turn))
+
+    @pl.when(has_far)
+    def _():
+        greet(source)
+
+        @pl.when(core == par)
+        def _():
+            greet(source + 1 - 2 * core)
 
     def remote(step, kind, src, dst, device):
         return pltpu.make_async_remote_copy(
@@ -116,12 +134,24 @@
             fld[c, rows] = piece
             win[c, 2, rows] = piece.astype(jnp.bfloat16)
 
-    pl.semaphore_wait(barrier, n - 1)
+    extra = jnp.where(has_onward, jnp.where(core == par, 1, 2), 0)
+    pl.semaphore_wait(barrier, (RADIX - 1) * len(strides) + extra)
 
     @pl.loop(0, chunks)
     def _(c):
         direct(c).start()
         own_to_sib(c).start()
+
+    def pass_on(step):
+        direct(step).wait_recv()
+
+        @pl.when(has_onward)
+        def _():
+            forward(step).start()
+
+        @pl.when(has_cousin)
+        def _():
+            relay(step).start()
 
     loads[1].wait()
 
@@ -131,6 +161,7 @@
         stacked = jnp.concatenate([w1_v[tap, rows, :] for tap in range(3)], axis=0)
         w1t[:, role * 3 * nvars : (role + 1) * 3 * nvars] = stacked.astype(jnp.float32).T.astype(jnp.bfloat16)
 
+    pass_on(0)
     b1t[...] = jnp.broadcast_to(b1_ref[...], (LANES, hid)).T
     b2t[...] = jnp.broadcast_to(b2_ref[...], (LANES, nvars)).T
     loads[2].wait()
@@ -157,6 +188,8 @@
         xf = x.astype(jnp.float32)
         return [pltpu.roll(xf, 1, 1).astype(jnp.bfloat16), x, pltpu.roll(xf, width - 1, 1).astype(jnp.bfloat16)]
 
+    lane = lax.broadcasted_iota(jnp.int32, (nvars, width), 1)
+    valid = jnp.logical_and(lane >= halo, lane < halo + useful)
     split = 2 * 3 * nvars
 
     def product(step, first, last, weights):
@@ -167,96 +200,88 @@
         own_to_sib(step).wait_recv()
         acc[c] = product(step, 0, 2, w1t[:, :split]) + b1t[:, :1]
 
+    def finish(step, c):
+        @pl.when(has_far)
+        def _():
+            forward(step).wait_recv()
+
+        @pl.when(jnp.logical_or(core != par, has_far))
+        def _():
+            relay(step).wait_recv()
+
+        pre = acc[c] + product(step, 2, 5, w1t[:, split:])
+        hidden = (0.5 * pre * (1.0 + jnp.tanh(0.5 * pre))).astype(jnp.bfloat16)
+        y = jnp.dot(w2_v[...].reshape(3 * nvars, hid), hidden, preferred_element_type=jnp.float32)
+        out = pltpu.roll(y[:nvars], 1, 1) + y[nvars : 2 * nvars] + pltpu.roll(y[2 * nvars :], width - 1, 1)
+        field = fld[c]
+        return field, out + b2t[:, :1] + inn[0, c] * (inn[1, c] - field)
+
+    @pl.loop(1, chunks)
+    def _(c):
+        begin(c - 1, c - 1)
+        pass_on(c)
+
+    begin(chunks - 1, chunks - 1)
+
     @pl.loop(0, chunks)
     def _(c):
-        begin(c, c)
-
-    lane = lax.broadcasted_iota(jnp.int32, (nvars, width), 1)
-    valid = jnp.logical_and(lane >= halo, lane < halo + useful)
-
-    @pl.loop(0, steps + 1)
-    def _(turn):
-        @pl.when(turn < steps)
-        def _():
-            direct(turn).wait_recv()
-
-            @pl.when(has_cousin)
-            def _():
-                relay(turn).start()
-
-            @pl.when(has_onward)
-            def _():
-                forward(turn).start()
-
-        @pl.when(turn >= 1)
-        def _():
-            step = turn - 1
-            c = lax.rem(step, chunks)
-
-            @pl.when(step >= chunks)
-            def _():
-                begin(step, c)
-
-            @pl.when(has_far)
-            def _():
-                forward(step).wait_recv()
-
-            @pl.when(jnp.logical_or(core != par, has_far))
-            def _():
-                relay(step).wait_recv()
-
-            pre = acc[c] + product(step, 2, 5, w1t[:, split:])
-            hidden = (0.5 * pre * (1.0 + jnp.tanh(0.5 * pre))).astype(jnp.bfloat16)
-            y = jnp.dot(w2_v[...].reshape(3 * nvars, hid), hidden, preferred_element_type=jnp.float32)
-            out = pltpu.roll(y[:nvars], 1, 1) + y[nvars : 2 * nvars] + pltpu.roll(y[2 * nvars :], width - 1, 1)
-            field = fld[c]
-            score = out + b2t[:, :1] + inn[0, c] * (inn[1, c] - field)
-
-            @pl.when(step < chunks)
-            def _():
-                moved = field + 0.5 * score
-                fld[c] = moved
-                win[step + chunks, 2] = moved.astype(jnp.bfloat16)
-                direct(step + chunks).start()
-                own_to_sib(step + chunks).start()
-
-            @pl.when(step >= chunks)
-            def _():
-                drift[c] = score
-                gacc[...] += jnp.where(valid, score * score, 0.0)
+        field, score = finish(c, c)
+        moved = field + 0.5 * score
+        fld[c] = moved
+        win[c + chunks, 2] = moved.astype(jnp.bfloat16)
+        direct(c + chunks).start()
+        own_to_sib(c + chunks).start()
+
+        @pl.when(c >= 1)
+        def _():
+            pass_on(c + chunks - 1)
+
+    @pl.loop(0, chunks - 1)
+    def _(c):
+        begin(c + chunks, c)
+
+    pass_on(steps - 1)
+    begin(steps - 1, chunks - 1)
+
+    @pl.loop(0, chunks)
+    def _(c):
+        _, score = finish(c + chunks, c)
+        drift[c] = score
+        gacc[...] += jnp.where(valid, score * score, 0.0)
 
     gsq = gacc[...]
-    row = lax.broadcasted_iota(jnp.int32, (8, LANES), 0)
-    sums[me] = jnp.where(row == 0, zsq, jnp.sum(gsq))
-
-    def share(device, slot):
+    def share(stage, turn):
+        stride = strides[stage]
         return pltpu.make_async_remote_copy(
-            src_ref=sums.at[me],
-            dst_ref=sums.at[slot],
-            send_sem=sum_send.at[device],
-            recv_sem=sum_recv.at[slot],
-            device_id=(group, device),
+            src_ref=sums.at[stage, 0],
+            dst_ref=sums.at[stage, turn],
+            send_sem=sum_send.at[stage, turn],
+            recv_sem=sum_recv.at[stage, turn],
+            device_id=(group, peer(stride, turn)),
             device_id_type=pl.DeviceIdType.MESH,
         )
 
-    @pl.loop(1, n)
-    def _(d):
-        share(lax.rem(me + d, n), me).start()
-
-    @pl.loop(0, nvars // ROWS)
-    def _(i):
-        rows = pl.ds(pl.multiple_of(i * ROWS, ROWS), ROWS)
-        for c in range(chunks):
-            span = slice(c * useful, (c + 1) * useful)
-            whole[0, rows, span] = fld[c, rows, halo : halo + useful]
-            whole[1, rows, span] = drift[c, rows, halo : halo + useful]
-
-    @pl.loop(1, n)
-    def _(d):
-        other = lax.rem(me + d, n)
-        share(other, other).wait_recv()
-
-    tot = jnp.sum(sums[...], axis=0)
+    row = lax.broadcasted_iota(jnp.int32, (8, LANES), 0)
+    tot = jnp.where(row == 0, zsq, jnp.sum(gsq))
+    for stage in range(len(strides)):
+        sums[stage, 0] = tot
+        for turn in range(1, RADIX):
+            share(stage, turn).start()
+
+        if stage == 0:
+
+            @pl.loop(0, nvars // ROWS)
+            def _(i):
+                rows = pl.ds(pl.multiple_of(i * ROWS, ROWS), ROWS)
+                for c in range(chunks):
+                    span = slice(c * useful, (c + 1) * useful)
+                    whole[0, rows, span] = fld[c, rows, halo : halo + useful]
+                    whole[1, rows, span] = drift[c, rows, halo : halo + useful]
+
+        for turn in range(1, RADIX):
+            share(stage, turn).wait_recv()
+        tot = (sums[stage, 0] + sums[stage, 2]) + (sums[stage, 1] + sums[stage, 3])
+
     zall = tot[0:1, 0:1]
     gall = tot[1:2, 0:1]
     size = 2.0 * 0.16 * 0.16 * zall / (gall + 1e-06)
@@ -267,9 +292,9 @@
         rows = pl.ds(pl.multiple_of(i * ROWS, ROWS), ROWS)
         out_ref[rows, 0, :] = whole[0, rows] + size * whole[1, rows] + scale * whole[2, rows]
 
-    @pl.loop(1, n)
-    def _(d):
-        share(lax.rem(me + d, n), me).wait_send()
+    for stage in range(len(strides)):
+        for turn in range(1, RADIX):
+            share(stage, turn).wait_send()
 
     @pl.loop(0, steps)
     def _(step):
@@ -301,6 +326,8 @@
     any_spec = pl.BlockSpec(memory_space=pl.ANY)
     vmem = pl.BlockSpec(memory_space=pltpu.VMEM)
     steps = 2 * chunks
+    stages = round(math.log(n, RADIX))
+    assert RADIX**stages == n
     flops = 4 * width * chunks * hid * nvars * (15 + 3)
     out = pl.pallas_call(
         functools.partial(kernel, n, chunks, useful, halo),
@@ -324,12 +351,12 @@
             pltpu.VMEM((chunks, hid, width), jnp.float32),
             pltpu.VMEM((3, nvars, lon), jnp.float32),
             pltpu.VMEM((steps, 5, nvars, width), jnp.bfloat16),
-            pltpu.VMEM((n, 8, LANES), jnp.float32),
+            pltpu.VMEM((stages, RADIX, 8, LANES), jnp.float32),
             pltpu.SemaphoreType.DMA((6,)),
             pltpu.SemaphoreType.DMA((steps, 4)),
             pltpu.SemaphoreType.DMA((steps, 4)),
-            pltpu.SemaphoreType.DMA((n,)),
-            pltpu.SemaphoreType.DMA((n,)),
+            pltpu.SemaphoreType.DMA((stages, RADIX)),
+            pltpu.SemaphoreType.DMA((stages, RADIX)),
         ],
         compiler_params=pltpu.CompilerParams(
             collective_id=0, has_side_effects=True, vmem_limit_bytes=62 * 1024 * 1024

time: 36.5 us -> 35 us (0.959)
  Pallas kernels: 34.5 us -> 33 us
    pallas_call x1, Pallas kernels: 34.5 us -> 33 us  [on_device(): pl.pallas_call(functools.partial(kernel, n, chunks, useful, halo), out_sh...]
where the time goes in v7:
time: 35 us; the launch traced here: 34.8 us
  Pallas kernels  33 us (94%)
  local copies, waits for them, and re-layouts  1.78 us (5%)
    pallas_call x1, Pallas kernels, on_device(): pl.pallas_call(functools.partial(kernel, n, chunks, useful, halo), out_sh...  33 us
    unnamed x1, local copies, waits for them, and re-layouts  1.78 us

profile of v7, /device:TPU:0, one launch (start us, length us, event | category | flops | bytes accessed | tf_op | source)
XLA Modules:
  0.0 34.8 jit_solution(5910680223552283477)
XLA Ops:
  0.0 33.0 %shard_map.82 = f32[64,1,1440]{2,1,0:T(1,128)} custom-call(f32[64,1,1440]{2,1,0:T(1,128)} %bitcast.11, f32[64,1,1440]{2,1,0:T(1,128)} %bitcast.12, s32[64,1,1440]{2,1,0:T(1,128)} %bitcast.13, f32[64,1,1440]{2,1,0:T(1,128)} %bitcast.14, bf16[3,3,320,256]{3,2,1,0:T(8,128)(2,1)} %bitcast.10, f32[1,256]{1,0:T(1,128)} %bitcast.16, ...), custom_call_target="tpu_custom_call" | custom-call | flops 1811939328 | bytes 4194304 | tf_op jit(solution)/shard_map/pallas_call | solution.py:332
  33.0 1.8 %copy.10 = f32[1,64,1,1440]{3,2,1,0:T(1,128)} copy(f32[1,64,1,1440]{3,2,1,0:T(1,128)} %bitcast.9) | data formatting | bytes 737280

commit v8 on v7

--- a/solution.py
+++ b/solution.py
@@ -8,7 +8,7 @@
 from jax.experimental.pallas import tpu as pltpu
 from jax.sharding import PartitionSpec as P
 
-CHUNKS = 3
+CHUNKS = 2
 LANES = 128
 ROWS = 16
 RADIX = 4

time: 35 us -> 36.3 us (1.037)
  Pallas kernels: 33 us -> 34.2 us
    pallas_call x1, Pallas kernels: 33 us -> 34.2 us  [on_device(): pl.pallas_call(functools.partial(kernel, n, chunks, useful, halo), out_sh...]
where the time goes in v8:
time: 36.3 us; the launch traced here: 36 us
  Pallas kernels  34.2 us (94%)
  local copies, waits for them, and re-layouts  1.78 us (5%)
    pallas_call x1, Pallas kernels, on_device(): pl.pallas_call(functools.partial(kernel, n, chunks, useful, halo), out_sh...  34.2 us
    unnamed x1, local copies, waits for them, and re-layouts  1.78 us

profile of v8, /device:TPU:0, one launch (start us, length us, event | category | flops | bytes accessed | tf_op | source)
XLA Modules:
  0.0 36.0 jit_solution(14033849420701120260)
XLA Ops:
  0.0 34.2 %shard_map.82 = f32[64,1,1440]{2,1,0:T(1,128)} custom-call(f32[64,1,1440]{2,1,0:T(1,128)} %bitcast.11, f32[64,1,1440]{2,1,0:T(1,128)} %bitcast.12, s32[64,1,1440]{2,1,0:T(1,128)} %bitcast.13, f32[64,1,1440]{2,1,0:T(1,128)} %bitcast.14, bf16[3,3,320,256]{3,2,1,0:T(8,128)(2,1)} %bitcast.10, f32[1,256]{1,0:T(1,128)} %bitcast.16, ...), custom_call_target="tpu_custom_call" | custom-call | flops 1811939328 | bytes 4194304 | tf_op jit(solution)/shard_map/pallas_call | solution.py:332
  34.3 1.8 %copy.10 = f32[1,64,1,1440]{3,2,1,0:T(1,128)} copy(f32[1,64,1,1440]{3,2,1,0:T(1,128)} %bitcast.9) | data formatting | bytes 737280
